TPU v7x, 512 devices: a whole 4x8x8 slice. The times are simulated.
512 devices in a mesh: patch: 512 (over z, x, y, core).
Axes of the slice: x: 4, y: 8, z: 8, core: 2. Of those that a mesh axis runs over, the one named last changes fastest.
Arguments:
- inputs: bfloat16 [1536, 32, 32, 128], P('patch'), may hold values from -6 to 6
- cotangent: bfloat16 [1536, 32, 32, 128], P('patch'), may hold values from -6 to 6
- weights: bfloat16 [3, 3, 128, 128], replicated, may hold values from -0.1875 to 0.1875
- bias_vector: float32 [128], replicated, may hold values from -3 to 3
- neighbours: int32 [1536, 8], P('patch'), may hold values from 0 to 1535, as said below
- rotations: int32 [1536, 8], P('patch'), may hold values from 0 to 3
- corners: int32 [1536, 8], P('patch'), may hold values from 0 to 1, as said below
Outputs:
- outputs: bfloat16 [1536, 32, 32, 128], P('patch')
- input_grad: bfloat16 [1536, 32, 32, 128], P('patch')
- weight_grad: float32 [3, 3, 128, 128], replicated
- bias_grad: float32 [128], replicated
Inputs may be any that keep to these rules, and one draw needn't show every extreme that they name: `neighbours`: the neighbour of a patch on device d lies on a device d + o (modulo the device count) with |o| <= 2; offsets 2 and -2 both occur. `corners`: the four side directions are always 1.
All inputs are finite; a program needn't handle non-finite values.
Results may differ from a plain program's by a relative error of at most 0.0035.
Values may be sent and summed in bfloat16 or wider, within the bound.
A program may use at most 64 MiB of HBM per device.

v0:
```python
import math

import jax
import jax.numpy as jnp
from jax import lax
from jax.sharding import PartitionSpec as P

REACH = 2


DIRECTIONS = ((-1, -1), (-1, 0), (-1, 1), (0, -1), (0, 1), (1, -1), (1, 0), (1, 1))
SIDE_TABLE = (
    ((0, 0), (3, 1), (1, 3), (2, 2)),
    ((1, 0), (2, 1), (0, 3), (3, 2)),
    ((2, 0), (0, 2), (3, 3), (1, 1)),
    ((3, 0), (1, 2), (2, 3), (0, 1)),
)


def passed_along(value, axis, steps):
    count = lax.axis_size(axis)
    pairs = [(source, (source + steps) % count) for source in range(count)]
    return lax.ppermute(value, axis, pairs)


def aligned_span(step, length):
    if step < 0:
        return slice(length - 2, length)
    if step == 0:
        return slice(0, length)
    return slice(0, 2)


def outer_span(step, length):
    if step < 0:
        return slice(0, 2)
    if step == 0:
        return slice(2, length + 2)
    return slice(length + 2, length + 4)


def aligned_pad(step, length):
    if step < 0:
        return (length - 2, 0)
    if step == 0:
        return (0, 0)
    return (0, length - 2)


def wanted_side(row_step, col_step):
    if row_step < 0:
        return 1
    if row_step > 0:
        return 0
    if col_step < 0:
        return 3
    return 2


def side_views(patches):
    length = patches.shape[1]
    upper = patches[:, 0:2]
    lower = patches[:, length - 2 :]
    left_cols = jnp.swapaxes(patches[:, :, 0:2], 1, 2)
    right_cols = jnp.swapaxes(patches[:, :, length - 2 :], 1, 2)
    return jnp.stack([upper, lower, left_cols, right_cols], axis=1)


def flip_side(strip, code):
    if code & 1:
        strip = strip[:, ::-1]
    if code & 2:
        strip = strip[:, :, ::-1]
    return strip


def turned_side(sides, quarter, which):
    turns = quarter[:, None, None, None]
    result = None
    for k in range(4):
        slot, code = SIDE_TABLE[which][k]
        candidate = flip_side(sides[:, slot], code)
        result = candidate if result is None else jnp.where(turns == k, candidate, result)
    return result


def extend_patch(center, gathered, rotations, corners):
    pieces = {}
    length = center.shape[1]
    for j, (row_step, col_step) in enumerate(DIRECTIONS):
        strip = turned_side(gathered[:, j], rotations[:, j], wanted_side(row_step, col_step))
        if row_step != 0:
            region = strip[:, :, aligned_span(col_step, length)]
        else:
            region = jnp.swapaxes(strip, 1, 2)
        present = corners[:, j][:, None, None, None] > 0
        pieces[row_step, col_step] = jnp.where(present, region, jnp.zeros_like(region))
    upper = jnp.concatenate([pieces[-1, -1], pieces[-1, 0], pieces[-1, 1]], axis=2)
    middle = jnp.concatenate([pieces[0, -1], center, pieces[0, 1]], axis=2)
    lower = jnp.concatenate([pieces[1, -1], pieces[1, 0], pieces[1, 1]], axis=2)
    return jnp.concatenate([upper, middle, lower], axis=1)


def dilated_conv(extended, kernel):
    return lax.conv_general_dilated(
        extended,
        kernel,
        (1, 1),
        "VALID",
        rhs_dilation=(2, 2),
        dimension_numbers=("NHWC", "HWIO", "NHWC"),
        preferred_element_type=jnp.float32,
    )


def collect_edges(strips):
    blocks = {0: strips}
    for offset in range(-REACH, REACH + 1):
        if offset != 0:
            blocks[offset] = passed_along(strips, "patch", -offset)
    return jnp.concatenate([blocks[offset] for offset in range(-REACH, REACH + 1)], axis=0)


def deliver_terms(pooled, patches_here):

    def member(offset):
        start = (offset + REACH) * patches_here
        return pooled[start : start + patches_here]

    total = member(0)
    for offset in range(-REACH, REACH + 1):
        if offset != 0:
            total = total + passed_along(
                member(offset).astype(jnp.bfloat16), "patch", offset
            ).astype(jnp.float32)
    return total


def side_terms(region, quarter, which):
    turns = quarter[:, None, None, None]
    slots = [None, None, None, None]
    for k in range(4):
        slot, code = SIDE_TABLE[which][k]
        slots[slot] = jnp.where(turns == k, flip_side(region, code), jnp.zeros_like(region))
    return jnp.stack(slots, axis=1)


def body(inputs, cotangent, weights, bias_vector, neighbours, rotations, corners):
    patches_here, length, _, chans = inputs.shape
    devices_all = lax.axis_size("patch")
    own_index = lax.axis_index("patch")
    owners = neighbours // patches_here
    offset = (owners - own_index) % devices_all
    offset = jnp.where(offset > devices_all // 2, offset - devices_all, offset)
    places = (offset + REACH) * patches_here + neighbours % patches_here
    pooled_edges = collect_edges(side_views(inputs))
    gathered = pooled_edges[places]
    extended = extend_patch(inputs, gathered, rotations, corners)
    outputs = (dilated_conv(extended, weights) + bias_vector).astype(jnp.bfloat16)
    padded_grad = jnp.pad(cotangent, ((0, 0), (4, 4), (4, 4), (0, 0)))
    flipped = jnp.swapaxes(weights[::-1, ::-1], 2, 3)
    ext_grad = dilated_conv(padded_grad, flipped)
    parts = []
    for j, (row_step, col_step) in enumerate(DIRECTIONS):
        region = ext_grad[:, outer_span(row_step, length), outer_span(col_step, length)]
        present = corners[:, j][:, None, None, None] > 0
        region = jnp.where(present, region, jnp.zeros_like(region))
        if row_step != 0:
            region = jnp.pad(region, ((0, 0), (0, 0), aligned_pad(col_step, length), (0, 0)))
        else:
            region = jnp.swapaxes(region, 1, 2)
        parts.append(side_terms(region, rotations[:, j], wanted_side(row_step, col_step)))
    returned = jnp.stack(parts, axis=1)
    pooled_terms = jnp.zeros(((2 * REACH + 1) * patches_here,) + returned.shape[2:], jnp.float32)
    pooled_terms = pooled_terms.at[places.reshape(-1)].add(
        returned.reshape((-1,) + returned.shape[2:])
    )
    arrived = deliver_terms(pooled_terms, patches_here)
    rest = length - 2
    added = jnp.pad(arrived[:, 0], ((0, 0), (0, rest), (0, 0), (0, 0)))
    added = added + jnp.pad(arrived[:, 1], ((0, 0), (rest, 0), (0, 0), (0, 0)))
    added = added + jnp.pad(jnp.swapaxes(arrived[:, 2], 1, 2), ((0, 0), (0, 0), (0, rest), (0, 0)))
    added = added + jnp.pad(jnp.swapaxes(arrived[:, 3], 1, 2), ((0, 0), (0, 0), (rest, 0), (0, 0)))
    input_grad = (ext_grad[:, 2 : length + 2, 2 : length + 2] + added).astype(jnp.bfloat16)
    taps = []
    for a in range(3):
        for b in range(3):
            window = extended[:, 2 * a : 2 * a + length, 2 * b : 2 * b + length]
            taps.append(
                jnp.einsum("pijc,pijd->cd", window, cotangent, preferred_element_type=jnp.float32)
            )
    weight_local = jnp.stack(taps, axis=0).reshape(3, 3, chans, chans)
    bias_local = jnp.sum(cotangent.astype(jnp.float32), axis=(0, 1, 2))
    weight_total, bias_total = lax.psum((weight_local, bias_local), "patch")
    factor = 1.0 / (length * math.sqrt(patches_here * devices_all))
    return (outputs, input_grad, weight_total * factor, bias_total * factor)


def solution(mesh):
    in_specs = (
        P("patch", None, None, None),
        P("patch", None, None, None),
        P(),
        P(),
        P("patch", None),
        P("patch", None),
        P("patch", None),
    )
    out_specs = (P("patch", None, None, None), P("patch", None, None, None), P(), P())
    return jax.shard_map(body, mesh=mesh, in_specs=in_specs, out_specs=out_specs, check_vma=False)
```

profile of v0, /device:TPU:1, one launch (start us, length us, event | category | flops | bytes accessed | tf_op | source)
XLA Modules:
  0.0 477.8 jit_solution(4005910151209333247)
XLA Ops:
  7.2 1.1 fusion.96
  8.4 0.8 slice_bitcast_fusion.36
  9.2 0.7 pad_maximum_fusion.4
  9.9 4.0 collective-permute-start
  14.0 4.0 collective-permute-start.1
  18.0 4.5 collective-permute-start.2
  22.6 10.4 %collective-permute-start.3 = (bf16[3,4,2,32,128]{4,3,2,1,0:T(8,128)(2,1)}, bf16[3,4,2,32,128]{4,3,2,1,0:T(8,128)(2,1)}, u32[]{:S(2)}, u32[]{:S(2)}) collective-permute-start(bf16[3,4,2,32,128]{4,3,2,1,0:T(8,128)(2,1)} %pad_maximum_fusion.4), channel_id=1, source_target_pairs={{0,510},{1,511},{2,0},{3,1},{4,2},{5,3},{6,4},{7,5},{8,6},{9,7},{1... | collective-permute-start | bytes 589832 | tf_op jit(solution)/shard_map/ppermute | solution.py:23
  33.0 2.3 compare_reduce_fusion
  35.3 1.3 fusion.77
  36.6 1.4 copy.230
  38.8 3.3 fusion.11
  43.3 1.0 select_bitcast_fusion.22
  45.6 0.8 select_bitcast_fusion.7
  49.0 0.8 select_bitcast_fusion.13
  52.4 1.4 select_bitcast_fusion.3
  54.2 0.7 select_bitcast_fusion.19
  54.9 0.7 select_bitcast_fusion.14
  55.9 1.0 select_bitcast_fusion.28
  56.8 1.0 select_bitcast_fusion.31
  57.8 1.0 select_bitcast_fusion.20
  58.8 1.0 select_bitcast_fusion.23
  59.8 0.7 select_bitcast_fusion.17
  60.5 1.0 select_bitcast_fusion.18
  61.5 0.8 select_bitcast_fusion.12
  62.2 1.0 select_bitcast_fusion.15
  65.0 2.0 copy.116
  67.3 6.1 %scatter_fusion = f32[15,4,2,32,128]{4,3,2,1,0:T(8,128)S(1)} fusion(f32[15,4,2,32,128]{4,3,2,1,0:T(8,128)S(1)} %broadcast_in_dim.359, s32[24]{0:T(128)S(1)} %fusion.86, f32[24,4,2,32,128]{4,3,2,1,0:T(8,128)} %bitcast.362), kind=kCustom, calls=%fused_computation.1 | custom fusion | flops 786432 | bytes 9437280 | tf_op jit(solution)/shard_map/scatter-add | solution.py:175
  73.4 1.5 copy.216
  75.0 1.4 fusion.95
  76.4 3.6 collective-permute-start.4
  80.5 94.4 %psum.15 = f32[128]{0:T(128)S(1)} all-reduce(f32[128]{0:T(128)S(1)} %convert_reduce_fusion), channel_id=1, replica_groups=mesh['patch'=512] {'patch'}, use_global_device_ids=true, to_apply=%region_3.4 | all-reduce | flops 128 | bytes 1024 | tf_op jit(solution)/shard_map/psum | solution.py:194
  175.4 2.8 copy.117
  178.3 2.6 collective-permute-start.5
  180.9 0.9 constant_dynamic-update-slice_fusion.4
  181.9 3.1 collective-permute-start.6
  184.9 1.0 constant_dynamic-update-slice_fusion.3
  186.0 3.1 collective-permute-start.7
  189.0 1.0 constant_dynamic-update-slice_fusion.1
  190.0 1.0 constant_dynamic-update-slice_fusion
  191.0 0.8 gather_fusion
  194.4 2.7 maximum_maximum_fusion.1
  200.9 0.8 copy-done.6
  202.4 1.7 fusion.35
  205.3 2.7 add_convert_fusion
  208.3 1.0 copy.136
  209.5 1.2 copy.135
  210.7 258.3 %all-reduce.10.cloned.1.call-done = f32[3,3,128,128]{3,2,1,0:T(8,128)} async-done(((f32[3,3,128,128]{3,2,1,0:T(8,128)}), f32[3,3,128,128]{3,2,1,0:T(8,128)}) %all-reduce.10.cloned.1.call-update) | async-done | bytes 589840 | tf_op jit(solution)/shard_map/psum | solution.py:194
  469.0 1.9 broadcast_multiply_fusion
  (232 shorter events, 20.1 us)
Async XLA Ops:
  7.2 31.4 %copy-start = (bf16[3,3,128,128]{3,2,1,0:T(8,128)(2,1)S(1)}, bf16[3,3,128,128]{3,2,1,0:T(8,128)(2,1)}, u32[]{:S(2)}) copy-start(bf16[3,3,128,128]{3,2,1,0:T(8,128)(2,1)} %param.9) | copy-start | bytes 884740
  7.2 461.9 %all-reduce.10.cloned.1.call-start = ((), (), s32[]{:S(2)}) async-start(), calls=%async_computation | async-start | bytes 1179648 | tf_op jit(solution)/shard_map/psum | solution.py:194
  9.9 168.4 %collective-permute-start = (bf16[3,4,2,32,128]{4,3,2,1,0:T(8,128)(2,1)}, bf16[3,4,2,32,128]{4,3,2,1,0:T(8,128)(2,1)}, u32[]{:S(2)}, u32[]{:S(2)}) collective-permute-start(bf16[3,4,2,32,128]{4,3,2,1,0:T(8,128)(2,1)} %pad_maximum_fusion.4), channel_id=1, source_target_pairs={{0,2},{1,3},{2,4},{3,5},{4,6},{5,7},{6,8},{7,9},{8,10},{9,11},{10,... | collective-permute-start | bytes 589832 | tf_op jit(solution)/shard_map/ppermute | solution.py:23
  14.0 167.9 %collective-permute-start.1 = (bf16[3,4,2,32,128]{4,3,2,1,0:T(8,128)(2,1)}, bf16[3,4,2,32,128]{4,3,2,1,0:T(8,128)(2,1)}, u32[]{:S(2)}, u32[]{:S(2)}) collective-permute-start(bf16[3,4,2,32,128]{4,3,2,1,0:T(8,128)(2,1)} %pad_maximum_fusion.4), channel_id=1, source_target_pairs={{0,1},{1,2},{2,3},{3,4},{4,5},{5,6},{6,7},{7,8},{8,9},{9,10},{10,1... | collective-permute-start | bytes 589832 | tf_op jit(solution)/shard_map/ppermute | solution.py:23
  18.0 167.9 %collective-permute-start.2 = (bf16[3,4,2,32,128]{4,3,2,1,0:T(8,128)(2,1)}, bf16[3,4,2,32,128]{4,3,2,1,0:T(8,128)(2,1)}, u32[]{:S(2)}, u32[]{:S(2)}) collective-permute-start(bf16[3,4,2,32,128]{4,3,2,1,0:T(8,128)(2,1)} %pad_maximum_fusion.4), channel_id=1, source_target_pairs={{0,511},{1,0},{2,1},{3,2},{4,3},{5,4},{6,5},{7,6},{8,7},{9,8},{10,... | collective-permute-start | bytes 589832 | tf_op jit(solution)/shard_map/ppermute | solution.py:23
  22.6 167.4 %collective-permute-start.3 = (bf16[3,4,2,32,128]{4,3,2,1,0:T(8,128)(2,1)}, bf16[3,4,2,32,128]{4,3,2,1,0:T(8,128)(2,1)}, u32[]{:S(2)}, u32[]{:S(2)}) collective-permute-start(bf16[3,4,2,32,128]{4,3,2,1,0:T(8,128)(2,1)} %pad_maximum_fusion.4), channel_id=1, source_target_pairs={{0,510},{1,511},{2,0},{3,1},{4,2},{5,3},{6,4},{7,5},{8,6},{9,7},{1... | collective-permute-start | bytes 589832 | tf_op jit(solution)/shard_map/ppermute | solution.py:23
  36.5 6.7 %copy-start.19 = (pred[3]{0:T(512)(128)(4,1)}, pred[3]{0:T(512)(128)(4,1)S(1)}, u32[]{:S(2)}) copy-start(pred[3]{0:T(512)(128)(4,1)S(1)} %get-tuple-element.49) | copy-start | bytes 13
  36.5 6.7 %copy-start.21 = (pred[3]{0:T(512)(128)(4,1)}, pred[3]{0:T(512)(128)(4,1)S(1)}, u32[]{:S(2)}) copy-start(pred[3]{0:T(512)(128)(4,1)S(1)} %get-tuple-element.54) | copy-start | bytes 13
  36.5 6.7 %copy-start.23 = (pred[3]{0:T(512)(128)(4,1)}, pred[3]{0:T(512)(128)(4,1)S(1)}, u32[]{:S(2)}) copy-start(pred[3]{0:T(512)(128)(4,1)S(1)} %get-tuple-element.48) | copy-start | bytes 13
  36.6 6.7 %copy-start.25 = (pred[3]{0:T(512)(128)(4,1)}, pred[3]{0:T(512)(128)(4,1)S(1)}, u32[]{:S(2)}) copy-start(pred[3]{0:T(512)(128)(4,1)S(1)} %get-tuple-element.52) | copy-start | bytes 13
  36.6 9.0 %copy-start.43 = (pred[3]{0:T(512)(128)(4,1)}, pred[3]{0:T(512)(128)(4,1)S(1)}, u32[]{:S(2)}) copy-start(pred[3]{0:T(512)(128)(4,1)S(1)} %get-tuple-element.55) | copy-start | bytes 13
  36.6 9.0 %copy-start.47 = (pred[3]{0:T(512)(128)(4,1)}, pred[3]{0:T(512)(128)(4,1)S(1)}, u32[]{:S(2)}) copy-start(pred[3]{0:T(512)(128)(4,1)S(1)} %get-tuple-element.53) | copy-start | bytes 13
  36.6 12.4 %copy-start.41 = (pred[3]{0:T(512)(128)(4,1)}, pred[3]{0:T(512)(128)(4,1)S(1)}, u32[]{:S(2)}) copy-start(pred[3]{0:T(512)(128)(4,1)S(1)} %get-tuple-element.50) | copy-start | bytes 13
  36.6 12.4 %copy-start.45 = (pred[3]{0:T(512)(128)(4,1)}, pred[3]{0:T(512)(128)(4,1)S(1)}, u32[]{:S(2)}) copy-start(pred[3]{0:T(512)(128)(4,1)S(1)} %get-tuple-element.51) | copy-start | bytes 13
  43.2 10.6 %copy-start.1 = (f32[36,3,36,128]{3,2,1,0:T(8,128)}, f32[36,3,36,128]{3,2,1,0:T(8,128)S(1)}, u32[]{:S(2)}) copy-start(f32[36,3,36,128]{3,2,1,0:T(8,128)S(1)} %copy.229) | copy-start | bytes 5971972
  53.8 8.4 %copy-start.28 = (pred[3]{0:T(512)(128)(4,1)S(1)}, pred[3]{0:T(512)(128)(4,1)}, u32[]{:S(2)}) copy-start(pred[3]{0:T(512)(128)(4,1)} %get-tuple-element.30) | copy-start | bytes 13
  53.8 6.0 %copy-start.16 = (f32[3,2,32,128]{3,2,0,1:T(8,128)S(1)}, f32[3,2,32,128]{3,2,0,1:T(8,128)}, u32[]{:S(2)}) copy-start(f32[3,2,32,128]{3,2,0,1:T(8,128)} %rev.196) | copy-start | bytes 294916
  53.8 7.7 %copy-start.15 = (f32[3,2,32,128]{3,2,0,1:T(8,128)S(1)}, f32[3,2,32,128]{3,2,0,1:T(8,128)}, u32[]{:S(2)}) copy-start(f32[3,2,32,128]{3,2,0,1:T(8,128)} %rev.199) | copy-start | bytes 294916
  53.9 9.6 %copy-start.18 = (f32[3,2,32,128]{3,2,0,1:T(8,128)S(1)}, f32[3,2,32,128]{3,2,0,1:T(8,128)}, u32[]{:S(2)}) copy-start(f32[3,2,32,128]{3,2,0,1:T(8,128)} %rev.188) | copy-start | bytes 294916
  53.9 9.6 %copy-start.33 = (pred[3]{0:T(512)(128)(4,1)S(1)}, pred[3]{0:T(512)(128)(4,1)}, u32[]{:S(2)}) copy-start(pred[3]{0:T(512)(128)(4,1)} %get-tuple-element.20) | copy-start | bytes 13
  53.9 9.6 %copy-start.35 = (pred[3]{0:T(512)(128)(4,1)S(1)}, pred[3]{0:T(512)(128)(4,1)}, u32[]{:S(2)}) copy-start(pred[3]{0:T(512)(128)(4,1)} %get-tuple-element.21) | copy-start | bytes 13
  54.0 9.7 %copy-start.29 = (pred[3]{0:T(512)(128)(4,1)S(1)}, pred[3]{0:T(512)(128)(4,1)}, u32[]{:S(2)}) copy-start(pred[3]{0:T(512)(128)(4,1)} %get-tuple-element.132) | copy-start | bytes 13
  54.0 9.7 %copy-start.31 = (pred[3]{0:T(512)(128)(4,1)S(1)}, pred[3]{0:T(512)(128)(4,1)}, u32[]{:S(2)}) copy-start(pred[3]{0:T(512)(128)(4,1)} %get-tuple-element.142) | copy-start | bytes 13
  54.1 9.7 %copy-start.13 = (f32[3,1,2,32,128]{4,3,0,2,1:T(8,128)S(1)}, f32[3,1,2,32,128]{4,3,0,2,1:T(8,128)}, u32[]{:S(2)}) copy-start(f32[3,1,2,32,128]{4,3,0,2,1:T(8,128)} %get-tuple-element.158) | copy-start | bytes 294916
  55.7 8.1 %copy-start.17 = (f32[3,2,32,128]{3,2,0,1:T(8,128)S(1)}, f32[3,2,32,128]{3,2,0,1:T(8,128)}, u32[]{:S(2)}) copy-start(f32[3,2,32,128]{3,2,0,1:T(8,128)} %rev.190) | copy-start | bytes 294916
  55.8 8.1 %copy-start.32 = (pred[3]{0:T(512)(128)(4,1)S(1)}, pred[3]{0:T(512)(128)(4,1)}, u32[]{:S(2)}) copy-start(pred[3]{0:T(512)(128)(4,1)} %get-tuple-element.143) | copy-start | bytes 13
  55.8 8.1 %copy-start.39 = (pred[3]{0:T(512)(128)(4,1)S(1)}, pred[3]{0:T(512)(128)(4,1)}, u32[]{:S(2)}) copy-start(pred[3]{0:T(512)(128)(4,1)} %get-tuple-element.135) | copy-start | bytes 13
  56.8 7.1 %copy-start.9 = (f32[3,1,2,32,128]{4,3,0,2,1:T(8,128)S(1)}, f32[3,1,2,32,128]{4,3,0,2,1:T(8,128)}, u32[]{:S(2)}) copy-start(f32[3,1,2,32,128]{4,3,0,2,1:T(8,128)} %get-tuple-element.70) | copy-start | bytes 294916
  60.5 3.5 copy-start.11
  63.3 0.9 copy-start.10
  63.5 0.9 copy-start.8
  63.8 0.9 copy-start.14
  63.8 0.9 copy-start.7
  64.0 0.9 copy-start.12
  65.0 2.0 copy-start.49
  73.4 6.6 %copy-start.4 = (bf16[3,32,32,128]{3,2,1,0:T(8,128)(2,1)S(1)}, bf16[3,32,32,128]{3,2,1,0:T(8,128)(2,1)}, u32[]{:S(2)}) copy-start(bf16[3,32,32,128]{3,2,1,0:T(8,128)(2,1)} %param.8) | copy-start | bytes 2359300
  76.4 125.9 %collective-permute-start.4 = (bf16[3,4,2,32,128]{4,2,0,3,1:T(2,128)(2,1)}, bf16[3,4,2,32,128]{4,2,0,3,1:T(2,128)(2,1)}, u32[]{:S(2)}, u32[]{:S(2)}) collective-permute-start(bf16[3,4,2,32,128]{4,2,0,3,1:T(2,128)(2,1)} %get-tuple-element.82), channel_id=1, source_target_pairs={{0,510},{1,511},{2,0},{3,1},{4,2},{5,3},{6,4},{7,5},{8,6},{9,7},{1... | collective-permute-start | bytes 589832 | tf_op jit(solution)/shard_map/ppermute | solution.py:23
  178.3 24.0 %collective-permute-start.5 = (bf16[3,4,2,32,128]{4,2,0,3,1:T(2,128)(2,1)}, bf16[3,4,2,32,128]{4,2,0,3,1:T(2,128)(2,1)}, u32[]{:S(2)}, u32[]{:S(2)}) collective-permute-start(bf16[3,4,2,32,128]{4,2,0,3,1:T(2,128)(2,1)} %get-tuple-element.85), channel_id=1, source_target_pairs={{0,511},{1,0},{2,1},{3,2},{4,3},{5,4},{6,5},{7,6},{8,7},{9,8},{10,... | collective-permute-start | bytes 589832 | tf_op jit(solution)/shard_map/ppermute | solution.py:23
  181.9 20.5 %collective-permute-start.6 = (bf16[3,4,2,32,128]{4,2,0,3,1:T(2,128)(2,1)}, bf16[3,4,2,32,128]{4,2,0,3,1:T(2,128)(2,1)}, u32[]{:S(2)}, u32[]{:S(2)}) collective-permute-start(bf16[3,4,2,32,128]{4,2,0,3,1:T(2,128)(2,1)} %get-tuple-element.84), channel_id=1, source_target_pairs={{0,1},{1,2},{2,3},{3,4},{4,5},{5,6},{6,7},{7,8},{8,9},{9,10},{10,1... | collective-permute-start | bytes 589832 | tf_op jit(solution)/shard_map/ppermute | solution.py:23
  186.0 16.4 %collective-permute-start.7 = (bf16[3,4,2,32,128]{4,2,0,3,1:T(2,128)(2,1)}, bf16[3,4,2,32,128]{4,2,0,3,1:T(2,128)(2,1)}, u32[]{:S(2)}, u32[]{:S(2)}) collective-permute-start(bf16[3,4,2,32,128]{4,2,0,3,1:T(2,128)(2,1)} %get-tuple-element.83), channel_id=1, source_target_pairs={{0,2},{1,3},{2,4},{3,5},{4,6},{5,7},{6,8},{7,9},{8,10},{9,11},{10,... | collective-permute-start | bytes 589832 | tf_op jit(solution)/shard_map/ppermute | solution.py:23
  192.6 0.9 copy-start.27
  192.6 0.9 copy-start.30
  192.6 0.9 copy-start.42
  192.6 0.9 copy-start.44
  193.2 0.8 copy-start.20
  193.2 1.1 copy-start.3
  193.8 3.3 copy-start.5
  205.3 2.7 copy-start.2
  (14 other events, 9.6 us)
Sparse Core Ops, SparseCore 0:
  201.9 267.1 all-reduce.9
where the time goes:
time: 479 us; the launch traced here: 478 us
  waiting for transfers between devices  258 us (54%)
  blocking collectives  94.4 us (20%)
  starting transfers between devices  35.4 us (7%)
  other arithmetic  33.7 us (7%)
  local copies, waits for them, and re-layouts  30.7 us (6%)
  between operations  15.4 us (3%)
  matrix products  9.83 us (2%)
    psum x1, waiting for transfers between devices, body(): weight_total, bias_total = lax.psum((weight_local, bias_local), 'patch')  258 us
    psum x1, blocking collectives, body(): weight_total, bias_total = lax.psum((weight_local, bias_local), 'patch')  94.4 us
    ppermute x8, starting transfers between devices, passed_along(): return lax.ppermute(value, axis, pairs)  35.4 us
    another operation x25, other arithmetic, side_terms(): return jnp.stack(slots, axis=1)  13.6 us
    unnamed x127, local copies, waits for them, and re-layouts  9.88 us
  transfers between devices with their start and end apart: 9, of which 1 were waited for; matrix products, arithmetic and copies ran while one was open for 14% of the time, Pallas kernels for 0%

commit v1 on v0

v1 whole, which is shorter than its diff:
```python
import functools
import math

import jax
import jax.numpy as jnp
from jax import lax
from jax.experimental import pallas as pl
from jax.experimental.pallas import tpu as pltpu
from jax.sharding import PartitionSpec as P

REACH = 2
MESH = pl.DeviceIdType.MESH
BF = jnp.bfloat16
F32 = jnp.float32
SIDE_TABLE = (
    ((0, 0), (3, 1), (1, 3), (2, 2)),
    ((1, 0), (2, 1), (0, 3), (3, 2)),
    ((2, 0), (0, 2), (3, 3), (1, 1)),
    ((3, 0), (1, 2), (2, 3), (0, 1)),
)
WANTED = (1, 1, 1, 3, 2, 0, 0, 0)
TORUS = {512: (8, 4, 8), 16: (2, 2, 2)}


def pick(k, values):
    out = jnp.int32(values[3])
    for i in (2, 1, 0):
        out = jnp.where(k == i, jnp.int32(values[i]), out)
    return out


def side_scalars(j, nb, rot, me, count, here):
    owner = nb // here
    off = lax.rem(owner - me + REACH + count, count)
    place = jnp.minimum(off, 2 * REACH) * here + (nb - owner * here)
    table = SIDE_TABLE[WANTED[j]]
    slot = pick(rot, [table[k][0] for k in range(4)])
    c1 = pick(rot, [table[k][1] & 1 for k in range(4)])
    c2 = pick(rot, [table[k][1] >> 1 for k in range(4)])
    return place * 4 + slot, c1, c2


def onehot(target, width):
    rows = target.shape[0]
    lanes = lax.broadcasted_iota(jnp.int32, (rows, width), 1)
    return jnp.where(lanes == target, 1.0, 0.0).astype(BF)


def rows_iota(rows):
    return lax.broadcasted_iota(jnp.int32, (rows, 1), 0)


def flip(c, x, last):
    return last * c + (1 - 2 * c) * x


def dot(a, b):
    return jnp.dot(a, b, preferred_element_type=F32)


def prepare_kernel(
    count, nb, rot, cor, inp, cot, wt, strips, terms, center, acc, zl, zr, cpad
):
    me = lax.axis_index("patch")
    here = inp.shape[0]
    acc[...] = jnp.zeros_like(acc)
    cpad[0:4] = jnp.zeros((4, 32, 128), BF)
    cpad[36:40] = jnp.zeros((4, 32, 128), BF)
    r64 = rows_iota(64)
    depth, along = r64 // 32, lax.rem(r64, 32)
    cols = lax.broadcasted_iota(jnp.int32, (6, 32, 128), 1)

    def patch(p, carry):
        strips[p * 4] = inp[p, 0:2].reshape(64, 128)
        strips[p * 4 + 1] = inp[p, 30:32].reshape(64, 128)
        left = inp[p, :, 0:16, :].reshape(512, 128)
        strips[p * 4 + 2] = dot(onehot(along * 16 + depth, 512), left).astype(BF)
        right = inp[p, :, 16:32, :].reshape(512, 128)
        strips[p * 4 + 3] = dot(onehot(along * 16 + depth + 14, 512), right).astype(BF)
        cpad[4:36] = cot[p]

        def chunk(n, c):
            y0 = n * 6
            lhs = jnp.concatenate(
                [cpad[pl.ds(y0 + 4 - 2 * a, 6)].reshape(192, 128) for a in range(3)],
                axis=1,
            )
            z = dot(lhs, wt[...])
            z0 = z[:, 0:128].reshape(6, 32, 128)
            z1 = z[:, 128:256].reshape(6, 32, 128)
            z2 = z[:, 256:384].reshape(6, 32, 128)
            zl[pl.ds(y0, 6)] = z0[:, 0:16].astype(BF)
            zr[pl.ds(y0, 6)] = z2[:, 16:32].astype(BF)
            total = z1 + jnp.where(cols < 30, pltpu.roll(z0, 30, 1), 0.0)
            total = total + jnp.where(cols >= 2, pltpu.roll(z2, 2, 1), 0.0)
            center[p, pl.ds(y0, 6)] = total
            return c

        lax.fori_loop(0, 6, chunk, 0)

        def back(j, target_of, block):
            row, c1, c2 = side_scalars(j, nb[p, j], rot[p, j], me, count, here)
            target = target_of(flip(c1, depth, 1), flip(c2, along, 31))
            target = jnp.where(cor[p, j] > 0, target, -1)
            acc[row] = acc[row] + dot(onehot(target, block.shape[0]), block)

        def last_two(step, q):
            return jnp.where(q >= 30, step + q - 30, -1)

        def first_two(step, q):
            return jnp.where(q < 2, step + 14 + q, -1)

        for base, rows in ((0, slice(0, 2)), (5, slice(34, 36))):
            mid = center[p, rows].reshape(64, 128).astype(BF)
            back(base, lambda r, q: last_two(16 * r, q), zl[rows].reshape(32, 128))
            back(base + 1, lambda r, q: 32 * r + q, mid)
            back(base + 2, lambda r, q: first_two(16 * r, q), zr[rows].reshape(32, 128))
        back(3, lambda c, i: 16 * i + c, zl[2:34].reshape(512, 128))
        back(4, lambda c, i: 16 * i + 14 + c, zr[2:34].reshape(512, 128))
        return carry

    lax.fori_loop(0, here, patch, 0)

    def narrow(n, c):
        terms[n] = acc[n].astype(BF)
        return c

    lax.fori_loop(0, terms.shape[0], narrow, 0)


def main_kernel(
    sizes,
    factor,
    nb,
    rot,
    cor,
    inp,
    cot,
    w,
    bias,
    strips,
    terms,
    center,
    out,
    ingrad,
    wgrad,
    bgrad,
    pool,
    arr,
    xs,
    cpad,
    wacc,
    wloc,
    core_out,
    core_in,
    y_out,
    y_in,
    z_out,
    z_in,
    x_all,
    z_all,
    fin,
    s_edge,
    r_edge,
    s_term,
    r_term,
    s_core,
    r_core,
    s_y,
    r_y,
    s_z,
    r_z,
    s_x,
    r_x,
    s_za,
    r_za,
    s_ya,
    r_ya,
    s_ca,
    r_ca,
):
    nz, nx, ny = sizes
    count = nz * nx * ny * 2
    me = lax.axis_index("patch")
    here = inp.shape[0]
    core = lax.rem(me, 2)
    y = lax.rem(me // 2, ny)
    x = lax.rem(me // (2 * ny), nx)
    z = me // (2 * ny * nx)
    mate = me + 1 - 2 * core
    block = here * 4
    zr, yr = wloc.shape[1] // nz, wloc.shape[1]

    def y_peer(k):
        yk = lax.rem(y + k, ny)
        return yk, me + 2 * (yk - y)

    def z_peer(k):
        zk = lax.rem(z + k, nz)
        return zk, me + 2 * ny * nx * (zk - z)

    def x_peer(k):
        xk = lax.rem(x + k, nx)
        return xk, me + 2 * ny * (xk - x)

    def near(o):
        return lax.rem(me + o + count, count)

    def copy(src, dst, send, recv, to):
        return pltpu.make_async_remote_copy(
            src_ref=src,
            dst_ref=dst,
            send_sem=send,
            recv_sem=recv,
            device_id=(to,),
            device_id_type=MESH,
        )

    barrier = pltpu.get_barrier_semaphore()
    peers = [mate]
    peers += [y_peer(k)[1] for k in range(1, ny)]
    peers += [z_peer(k)[1] for k in range(1, nz)]
    peers += [x_peer(k)[1] for k in range(1, nx)]
    peers += [near(o) for o in (-2, -1, 1, 2)]
    for peer in peers:
        pl.semaphore_signal(barrier, inc=1, device_id=(peer,), device_id_type=MESH)
    pl.semaphore_wait(barrier, len(peers))

    edges, backs = [], []
    for n, o in enumerate((-2, -1, 1, 2)):
        edges.append(
            copy(
                strips,
                pool.at[pl.ds((REACH - o) * block, block)],
                s_edge.at[n],
                r_edge.at[n],
                near(o),
            )
        )
        edges[-1].start()
    for n, o in enumerate((-2, -1, 1, 2)):
        backs.append(
            copy(
                terms.at[pl.ds((REACH + o) * block, block)],
                arr.at[n],
                s_term.at[n],
                r_term.at[n],
                near(o),
            )
        )
        backs[-1].start()
    pool[REACH * block : (REACH + 1) * block] = strips[...]

    cols = lax.broadcasted_iota(jnp.int32, (32, 32, 128), 1)

    def middle(p, total):
        here_in = inp[p]
        wide = here_in.astype(F32)
        xs[p, 2:34, :, 128:256] = here_in
        ahead = jnp.where(cols >= 2, pltpu.roll(wide, 2, 1), 0.0)
        xs[p, 2:34, :, 0:128] = ahead.astype(BF)
        behind = jnp.where(cols < 30, pltpu.roll(wide, 30, 1), 0.0)
        xs[p, 2:34, :, 256:384] = behind.astype(BF)
        cpad[p, 0:4] = jnp.zeros((4, 32, 128), BF)
        cpad[p, 36:40] = jnp.zeros((4, 32, 128), BF)
        here_cot = cot[p]
        cpad[p, 4:36] = here_cot
        return total + here_cot.astype(F32).reshape(128, 8, 128).sum(axis=0)

    bias8 = lax.fori_loop(0, here, middle, jnp.zeros((8, 128), F32))
    bias_here = jnp.sum(bias8, axis=0, keepdims=True)
    for c in edges:
        c.wait_recv()

    r192 = rows_iota(192)
    tap, depth, along = r192 // 64, lax.rem(r192 // 32, 2), lax.rem(r192, 32)
    at = 2 * tap + along
    r512 = rows_iota(512)
    line, place = r512 // 16, lax.rem(r512, 16)

    def halo(p, carry):
        def info(j):
            row, c1, c2 = side_scalars(j, nb[p, j], rot[p, j], me, count, here)
            return pool[row], c1, c2, cor[p, j] > 0

        for base, first in ((0, 0), (5, 34)):
            made = jnp.zeros((192, 128), F32)
            for j, q, inside in (
                (base, 30 + at, at < 2),
                (base + 1, at - 2, (at >= 2) & (at < 34)),
                (base + 2, at - 34, at >= 34),
            ):
                strip, c1, c2, present = info(j)
                target = 32 * flip(c1, depth, 1) + flip(c2, q, 31)
                target = jnp.where(inside & present, target, -1)
                made = made + dot(onehot(target, 64), strip)
            made = made.astype(BF)
            for b in range(3):
                piece = made[64 * b : 64 * b + 64].reshape(2, 32, 128)
                xs[p, first : first + 2, :, 128 * b : 128 * b + 128] = piece
        strip, c1, c2, present = info(3)
        target = 32 * flip(c1, place, 1) + flip(c2, line, 31)
        target = jnp.where((place < 2) & present, target, -1)
        made = dot(onehot(target, 64), strip).reshape(32, 16, 128)
        old = xs[p, 2:34, 0:16, 0:128].astype(F32)
        xs[p, 2:34, 0:16, 0:128] = (old + made).astype(BF)
        strip, c1, c2, present = info(4)
        target = 32 * flip(c1, place - 14, 1) + flip(c2, line, 31)
        target = jnp.where((place >= 14) & present, target, -1)
        made = dot(onehot(target, 64), strip).reshape(32, 16, 128)
        old = xs[p, 2:34, 16:32, 256:384].astype(F32)
        xs[p, 2:34, 16:32, 256:384] = (old + made).astype(BF)
        return carry

    lax.fori_loop(0, here, halo, 0)

    wacc[...] = jnp.zeros_like(wacc)

    def outer(n, carry):
        p, y0 = n // 3, lax.rem(n, 3) * 12
        lhs = xs[p, pl.ds(y0, 12)].reshape(384, 384)
        rhs = jnp.concatenate(
            [cpad[p, pl.ds(y0 + 4 - 2 * a, 12)].reshape(384, 128) for a in range(3)],
            axis=1,
        )
        wacc[...] += lax.dot_general(
            lhs, rhs, (((0,), (0,)), ((), ())), preferred_element_type=F32
        )
        return carry

    lax.fori_loop(0, here * 3, outer, 0)

    taps = [wacc[128 * b : 128 * b + 128, 128 * a : 128 * a + 128] for a in range(3) for b in range(3)]
    for s in range(2 * ny):
        lo, hi = s * yr, (s + 1) * yr
        while lo < hi:
            t = lo // 128
            end = min(hi, (t + 1) * 128)
            wloc[s, lo - s * yr : end - s * yr] = taps[t][lo - 128 * t : end - 128 * t]
            lo = end

    row8 = lax.broadcasted_iota(jnp.int32, (8, 128), 0)

    def bias_rows(b):
        top = b.astype(BF).astype(F32)
        return jnp.where(row8 == 0, top, jnp.where(row8 == 1, b - top, 0.0))

    def bias_of(rows):
        return rows[0:1] + rows[1:2]

    mine = bias_rows(bias_here)

    def to_mate(s, carry):
        core_out[s, 0:yr] = wloc[(1 - core) * ny + s].astype(BF)
        core_out[s, yr : yr + 8] = mine.astype(BF)
        return carry

    lax.fori_loop(0, ny, to_mate, 0)
    swap = copy(core_out, core_in, s_core, r_core, mate)
    swap.start()

    def conv(n, carry):
        p, i0 = n // 4, lax.rem(n, 4) * 8
        lhs = jnp.concatenate(
            [xs[p, pl.ds(i0 + 2 * a, 8)].reshape(256, 384) for a in range(3)], axis=1
        )
        out[p, pl.ds(i0, 8)] = (dot(lhs, w[...]) + bias[...]).astype(BF).reshape(8, 32, 128)
        return carry

    lax.fori_loop(0, 2, conv, 0)
    swap.wait_recv()

    def pair(s):
        data = wloc[core * ny + s] + core_in[s, 0:yr].astype(F32)
        return data, mine + core_in[s, yr : yr + 8].astype(F32)

    def to_line(s, carry):
        data, extra = pair(s)
        y_out[s, 0:yr] = data.astype(BF)
        y_out[s, yr : yr + 8] = bias_rows(bias_of(extra)).astype(BF)
        return carry

    lax.fori_loop(0, ny, to_line, 0)

    def y_reduce(k):
        yk, peer = y_peer(k)
        return copy(y_out.at[yk], y_in.at[k - 1], s_y.at[k - 1], r_y.at[k - 1], peer)

    for k in range(1, ny):
        y_reduce(k).start()
    lax.fori_loop(2, 8, conv, 0)
    data, extra = pair(y)
    for k in range(1, ny):
        y_reduce(k).wait_recv()
        data = data + y_in[k - 1, 0:yr].astype(F32)
        extra = extra + y_in[k - 1, yr : yr + 8].astype(F32)
    total_bias = bias_of(extra)
    z_out[...] = jnp.zeros_like(z_out)
    for zz in range(nz):
        z_out[zz, 0:zr] = data[zz * zr : (zz + 1) * zr]
        z_out[zz, zr : zr + 1] = total_bias

    def z_reduce(k):
        zk, peer = z_peer(k)
        return copy(z_out.at[zk], z_in.at[k - 1], s_z.at[k - 1], r_z.at[k - 1], peer)

    for k in range(1, nz):
        z_reduce(k).start()
    lax.fori_loop(8, 4 * here, conv, 0)
    data = z_out[z]
    for k in range(1, nz):
        z_reduce(k).wait_recv()
        data = data + z_in[k - 1]
    x_all[x] = data

    def x_gather(k):
        return copy(x_all.at[x], x_all.at[x], s_x.at[k - 1], r_x.at[k - 1], x_peer(k)[1])

    for k in range(1, nx):
        x_gather(k).start()
    for c in backs:
        c.wait_recv()

    def finish(p, carry):
        def arrived(slot):
            total = terms[REACH * block + p * 4 + slot].astype(F32)
            for n in range(4):
                total = total + arr[n, p * 4 + slot].astype(F32)
            return total.reshape(2, 32, 128)

        def columns(slot, shift):
            stack = [terms[REACH * block + p * 4 + slot]]
            stack += [arr[n, p * 4 + slot] for n in range(4)]
            spot = place - shift
            target = jnp.where((spot >= 0) & (spot < 2), 32 * spot + line, -1)
            spread = onehot(target, 64)
            made = jnp.zeros((512, 128), F32)
            for piece in stack:
                made = made + dot(spread, piece)
            return made.reshape(32, 16, 128)

        center[p, 2:34, 0:16] = center[p, 2:34, 0:16] + columns(2, 0)
        center[p, 2:34, 16:32] = center[p, 2:34, 16:32] + columns(3, 14)
        center[p, 2:4] = center[p, 2:4] + arrived(0)
        center[p, 32:34] = center[p, 32:34] + arrived(1)
        ingrad[p] = center[p, 2:34].astype(BF)
        return carry

    lax.fori_loop(0, here, finish, 0)
    for k in range(1, nx):
        x_gather(k).wait_recv()
    data = x_all[0]
    for n in range(1, nx):
        data = data + x_all[n]
    data = data * factor
    row_z = lax.broadcasted_iota(jnp.int32, data.shape, 0)
    b = data[zr : zr + 1]
    top = b.astype(BF).astype(F32)
    data = jnp.where(row_z == zr, top, jnp.where(row_z == zr + 1, b - top, data))
    z_all[z] = data.astype(BF)

    def z_gather(k):
        return copy(z_all.at[z], z_all.at[z], s_za.at[k - 1], r_za.at[k - 1], z_peer(k)[1])

    for k in range(1, nz):
        z_gather(k).start()
    for k in range(1, nz):
        z_gather(k).wait_recv()
    pieces = [z_all[zz].astype(F32) for zz in range(nz)]
    slab = jnp.concatenate([piece[0:zr] for piece in pieces], axis=0)
    spot = core * ny + y
    fin[spot, 0:yr] = slab.astype(BF)
    tail = pieces[0][zr : zr + 2]
    fin[spot, yr : yr + 8] = jnp.where(
        row8 == 0, tail[0:1], jnp.where(row8 == 1, tail[1:2], 0.0)
    ).astype(BF)

    def y_gather(k):
        return copy(fin.at[spot], fin.at[spot], s_ya.at[k - 1], r_ya.at[k - 1], y_peer(k)[1])

    def c_gather(k):
        at_y = core * ny + lax.rem(y - k + ny, ny)
        return copy(fin.at[at_y], fin.at[at_y], s_ca.at[k], r_ca.at[k], mate)

    for k in range(1, ny):
        y_gather(k).start()
    c_gather(0).start()
    for k in range(1, ny):
        y_gather(k).wait_recv()
        c_gather(k).start()
    for k in range(ny):
        c_gather(k).wait_recv()
    for s in range(2 * ny):
        wgrad[s * yr : (s + 1) * yr] = fin[s, 0:yr].astype(F32)
    tail = fin[0, yr : yr + 8].astype(F32)
    bgrad[...] = jnp.broadcast_to(bias_of(tail), bgrad.shape)

    for c in edges + backs + [swap]:
        c.wait_send()
    for k in range(1, ny):
        y_reduce(k).wait_send()
        y_gather(k).wait_send()
    for k in range(1, nz):
        z_reduce(k).wait_send()
        z_gather(k).wait_send()
    for k in range(1, nx):
        x_gather(k).wait_send()
    for k in range(ny):
        c_gather(k).wait_send()


def body(count, inputs, cotangent, weights, bias_vector, neighbours, rotations, corners):
    here, length, _, chans = inputs.shape
    sizes = TORUS[count]
    nz, nx, ny = sizes
    factor = 1.0 / (length * math.sqrt(here * count))
    block = here * 4
    smem = pl.BlockSpec(memory_space=pltpu.SMEM)
    vmem = pl.BlockSpec(memory_space=pltpu.VMEM)
    dma = pltpu.SemaphoreType.DMA
    turned = weights.transpose(0, 3, 1, 2).reshape(3 * chans, 3 * chans)
    strips, terms, center = pl.pallas_call(
        functools.partial(prepare_kernel, count),
        out_shape=(
            jax.ShapeDtypeStruct((block, 64, chans), BF),
            jax.ShapeDtypeStruct((5 * block, 64, chans), BF),
            jax.ShapeDtypeStruct((here, 36, 32, chans), F32),
        ),
        in_specs=[smem] * 3 + [vmem] * 3,
        out_specs=(vmem,) * 3,
        scratch_shapes=[
            pltpu.VMEM((5 * block, 64, chans), F32),
            pltpu.VMEM((36, 16, chans), BF),
            pltpu.VMEM((36, 16, chans), BF),
            pltpu.VMEM((40, 32, chans), BF),
        ],
        compiler_params=pltpu.CompilerParams(vmem_limit_bytes=40 * 2**20),
    )(neighbours, rotations, corners, inputs, cotangent, turned)

    yr = 9 * chans // (2 * ny)
    zr = yr // nz
    zpad = -(-(zr + 2) // 16) * 16
    outputs, input_grad, weight_grad, bias_grad = pl.pallas_call(
        functools.partial(main_kernel, sizes, factor),
        out_shape=(
            jax.ShapeDtypeStruct(inputs.shape, BF),
            jax.ShapeDtypeStruct(inputs.shape, BF),
            jax.ShapeDtypeStruct((9 * chans, chans), F32),
            jax.ShapeDtypeStruct((8, chans), F32),
        ),
        in_specs=[smem] * 3 + [vmem] * 7,
        out_specs=(vmem,) * 4,
        scratch_shapes=[
            pltpu.VMEM((5 * block, 64, chans), BF),
            pltpu.VMEM((4, block, 64, chans), BF),
            pltpu.VMEM((here, 36, 32, 3 * chans), BF),
            pltpu.VMEM((here, 40, 32, chans), BF),
            pltpu.VMEM((3 * chans, 3 * chans), F32),
            pltpu.VMEM((2 * ny, yr, chans), F32),
            pltpu.VMEM((ny, yr + 8, chans), BF),
            pltpu.VMEM((ny, yr + 8, chans), BF),
            pltpu.VMEM((ny, yr + 8, chans), BF),
            pltpu.VMEM((ny - 1, yr + 8, chans), BF),
            pltpu.VMEM((nz, zpad, chans), F32),
            pltpu.VMEM((nz - 1, zpad, chans), F32),
            pltpu.VMEM((nx, zpad, chans), F32),
            pltpu.VMEM((nz, zpad, chans), BF),
            pltpu.VMEM((2 * ny, yr + 8, chans), BF),
            dma((4,)),
            dma((4,)),
            dma((4,)),
            dma((4,)),
            dma,
            dma,
            dma((ny - 1,)),
            dma((ny - 1,)),
            dma((nz - 1,)),
            dma((nz - 1,)),
            dma((nx - 1,)),
            dma((nx - 1,)),
            dma((nz - 1,)),
            dma((nz - 1,)),
            dma((ny - 1,)),
            dma((ny - 1,)),
            dma((ny,)),
            dma((ny,)),
        ],
        compiler_params=pltpu.CompilerParams(
            collective_id=0, has_side_effects=True, vmem_limit_bytes=48 * 2**20
        ),
    )(
        neighbours,
        rotations,
        corners,
        inputs,
        cotangent,
        weights.reshape(9 * chans, chans),
        bias_vector.reshape(1, chans),
        strips,
        terms,
        center,
    )
    return (
        outputs,
        input_grad,
        weight_grad.reshape(3, 3, chans, chans),
        bias_grad[0],
    )


def solution(mesh):
    in_specs = (
        P("patch", None, None, None),
        P("patch", None, None, None),
        P(),
        P(),
        P("patch", None),
        P("patch", None),
        P("patch", None),
    )
    out_specs = (P("patch", None, None, None), P("patch", None, None, None), P(), P())
    return jax.shard_map(
        functools.partial(body, mesh.shape["patch"]),
        mesh=mesh,
        in_specs=in_specs,
        out_specs=out_specs,
        check_vma=False,
    )
```

time: 479 us -> 76.8 us (0.16)
  waiting for transfers between devices: 258 us -> 0 us
  blocking collectives: 94.4 us -> 0 us
  Pallas kernels: 0 us -> 66.9 us
  starting transfers between devices: 35.4 us -> 0 us
  other arithmetic: 33.7 us -> 0 us
  local copies, waits for them, and re-layouts: 30.7 us -> 8.85 us
  between operations: 15.4 us -> 0.76 us
  matrix products: 9.83 us -> 0 us
    psum x1 -> x0, waiting for transfers between devices: 258 us -> none  [body(): weight_total, bias_total = lax.psum((weight_local, bias_local), 'patch')]
    psum x1 -> x0, blocking collectives: 94.4 us -> none  [body(): weight_total, bias_total = lax.psum((weight_local, bias_local), 'patch')]
    pallas_call x0 -> x2, Pallas kernels: none -> 66.9 us  [the longest x1 59.9 us: body(): pl.pallas_call(functools.partial(main_kernel, sizes, factor), out_shape=(...]
    ppermute x8 -> x0, starting transfers between devices: 35.4 us -> none  [passed_along(): return lax.ppermute(value, axis, pairs)]
    another operation x27 -> x0, other arithmetic: 14.3 us -> none  [the longest x25 13.6 us: side_terms(): return jnp.stack(slots, axis=1)]
    rev x36 -> x0, local copies, waits for them, and re-layouts: 7.08 us -> none  [the longest x32 7.06 us: flip_side(): strip = strip[:, :, ::-1]]
    scatter-add x1 -> x0, other arithmetic: 6.11 us -> none  [body(): pooled_terms.at[places.reshape(-1)]]
    conv_general_dilated x2 -> x0, matrix products: 6.06 us -> none  [dilated_conv(): lax.conv_general_dilated(extended, kernel, (1, 1), 'VALID', rhs_dilation=...]
  transfers between devices with their start and end apart: 9 -> 0, of which waited for: 1 -> 0; matrix products, arithmetic and copies ran while one was open for 14% -> 0% of each run, Pallas kernels for 0% -> 0%
where the time goes in v1:
time: 76.8 us; the launch traced here: 76.5 us
  Pallas kernels  66.9 us (87%)
  local copies, waits for them, and re-layouts  8.85 us (12%)
    pallas_call x1, Pallas kernels, body(): pl.pallas_call(functools.partial(main_kernel, sizes, factor), out_shape=(...  59.9 us
    unnamed x28, local copies, waits for them, and re-layouts  7.05 us
    pallas_call x1, Pallas kernels, body(): pl.pallas_call(functools.partial(prepare_kernel, count), out_shape=(jax.S...  6.92 us

profile of v1, /device:TPU:1, one launch (start us, length us, event | category | flops | bytes accessed | tf_op | source)
XLA Modules:
  0.0 76.5 jit_solution(15216595633783901074)
XLA Ops:
  0.6 0.0 copy-start.10
  0.6 0.0 copy-start.8
  0.7 0.0 copy-start.6
  0.7 0.0 copy-start.4
  0.7 0.0 copy-start
  0.7 0.0 copy-start.11
  0.7 1.3 %copy.12 = bf16[3,128,3,128]{3,2,1,0:T(4,128)(2,1)S(1)} copy(bf16[3,128,3,128]{1,3,2,0:T(8,128)(2,1)} %bitcast.12) | data formatting | bytes 589824 | tf_op jit(solution)/shard_map/transpose | solution.py:521
  2.0 0.0 copy-done
  2.1 0.0 copy-start.1
  2.1 1.1 %copy-done.1 = bf16[3,32,32,128]{3,2,1,0:T(8,128)(2,1)S(1)} copy-done((bf16[3,32,32,128]{3,2,1,0:T(8,128)(2,1)S(1)}, bf16[3,32,32,128]{3,2,1,0:T(8,128)(2,1)}, u32[]{:S(2)}) %copy-start.1) | copy-done | bytes 786456
  3.2 0.0 copy-start.5
  3.2 0.7 copy-done.5
  3.9 0.0 copy-start.7
  3.9 0.7 copy-done.7
  4.6 0.0 copy-start.9
  4.6 0.7 copy-done.9
  5.2 0.0 copy-start.2
  5.2 6.9 %shard_map.102 = (bf16[12,64,128]{2,1,0:T(8,128)(2,1)S(1)}, bf16[60,64,128]{2,1,0:T(8,128)(2,1)S(1)}, f32[3,36,32,128]{3,2,1,0:T(8,128)S(1)}) custom-call(s32[3,8]{1,0:T(4,128)S(1)} %copy-done.5, s32[3,8]{1,0:T(4,128)S(1)} %copy-done.7, s32[3,8]{1,0:T(4,128)S(1)} %copy-done.9, bf16[3,32,32,128]{3,2,1,0:T(8,128)(2,1)S(1)} %copy-done, ...), custom_call_target="tpu_custom_call" | custom-call | tf_op jit(solution)/shard_map/pallas_call | solution.py:522
  12.2 0.0 copy-start.3
  12.2 1.2 %copy-done.3 = f32[3,36,32,128]{3,2,1,0:T(8,128)} copy-done((f32[3,36,32,128]{3,2,1,0:T(8,128)}, f32[3,36,32,128]{3,2,1,0:T(8,128)S(1)}, u32[]{:S(2)}) %copy-start.3) | copy-done | bytes 1769496
  13.4 0.0 copy-done.10
  13.4 0.0 copy-done.8
  13.4 0.0 copy-done.6
  13.4 0.0 copy-done.4
  13.4 0.0 copy-done.11
  13.4 0.0 copy-done.2
  13.4 59.9 %shard_map.103 = (bf16[3,32,32,128]{3,2,1,0:T(8,128)(2,1)S(1)}, bf16[3,32,32,128]{3,2,1,0:T(8,128)(2,1)S(1)}, f32[1152,128]{1,0:T(8,128)S(1)}, f32[8,128]{1,0:T(8,128)S(1)}) custom-call(s32[3,8]{1,0:T(4,128)S(1)} %copy-done.6, s32[3,8]{1,0:T(4,128)S(1)} %copy-done.8, s32[3,8]{1,0:T(4,128)S(1)} %copy-done.10, bf16[3,32,32,128]{3,2,1,0:T(8,128)(2,1)S(1)} %copy-done, ...), custom_call_target="tpu_custom_call" | custom-call | tf_op jit(solution)/shard_map/pallas_call | solution.py:543
  73.4 0.5 slice_bitcast_fusion
  73.9 0.9 %copy.19 = bf16[3,32,32,128]{3,2,1,0:T(8,128)(2,1)} copy(bf16[3,32,32,128]{3,2,1,0:T(8,128)(2,1)S(1)} %get-tuple-element.22) | data formatting | bytes 1572864
  74.8 0.9 %copy.20 = bf16[3,32,32,128]{3,2,1,0:T(8,128)(2,1)} copy(bf16[3,32,32,128]{3,2,1,0:T(8,128)(2,1)S(1)} %get-tuple-element.23) | data formatting | bytes 1572864
  75.7 0.8 %copy.21 = f32[3,3,128,128]{3,2,1,0:T(8,128)} copy(f32[3,3,128,128]{3,2,1,0:T(8,128)S(1)} %bitcast.14) | data formatting | bytes 1179648
  (1 shorter events, 0.0 us)
Async XLA Ops:
  0.6 12.8 %copy-start.10 = (s32[3,8]{1,0:T(4,128)S(1)}, s32[3,8]{1,0:T(4,128)}, u32[]{:S(2)}) copy-start(s32[3,8]{1,0:T(4,128)} %cor.3) | copy-start | bytes 292
  0.6 12.8 %copy-start.8 = (s32[3,8]{1,0:T(4,128)S(1)}, s32[3,8]{1,0:T(4,128)}, u32[]{:S(2)}) copy-start(s32[3,8]{1,0:T(4,128)} %rot.3) | copy-start | bytes 292
  0.7 12.8 %copy-start.6 = (s32[3,8]{1,0:T(4,128)S(1)}, s32[3,8]{1,0:T(4,128)}, u32[]{:S(2)}) copy-start(s32[3,8]{1,0:T(4,128)} %nb.3) | copy-start | bytes 292
  0.7 12.7 %copy-start.4 = (bf16[3,3,128,128]{3,2,1,0:T(8,128)(2,1)S(1)}, bf16[3,3,128,128]{3,2,1,0:T(8,128)(2,1)}, u32[]{:S(2)}) copy-start(bf16[3,3,128,128]{3,2,1,0:T(8,128)(2,1)} %param.9) | copy-start | bytes 884740
  0.7 1.4 %copy-start = (bf16[3,32,32,128]{3,2,1,0:T(8,128)(2,1)S(1)}, bf16[3,32,32,128]{3,2,1,0:T(8,128)(2,1)}, u32[]{:S(2)}) copy-start(bf16[3,32,32,128]{3,2,1,0:T(8,128)(2,1)} %inp.3) | copy-start | bytes 2359300
  0.7 12.7 %copy-start.11 = (f32[128]{0:T(128)S(1)}, f32[128]{0:T(128)}, u32[]{:S(2)}) copy-start(f32[128]{0:T(128)} %param.10) | copy-start | bytes 1540
  2.1 1.1 %copy-start.1 = (bf16[3,32,32,128]{3,2,1,0:T(8,128)(2,1)S(1)}, bf16[3,32,32,128]{3,2,1,0:T(8,128)(2,1)}, u32[]{:S(2)}) copy-start(bf16[3,32,32,128]{3,2,1,0:T(8,128)(2,1)} %cot.3) | copy-start | bytes 2359300
  3.2 0.7 copy-start.5
  3.9 0.7 copy-start.7
  4.6 0.7 copy-start.9
  5.2 8.2 %copy-start.2 = (bf16[3,32,32,128]{3,2,1,0:T(8,128)(2,1)S(1)}, bf16[3,32,32,128]{3,2,1,0:T(8,128)(2,1)}, u32[]{:S(2)}) copy-start(bf16[3,32,32,128]{3,2,1,0:T(8,128)(2,1)} %cot.3) | copy-start | bytes 2359300
  12.2 1.2 %copy-start.3 = (f32[3,36,32,128]{3,2,1,0:T(8,128)}, f32[3,36,32,128]{3,2,1,0:T(8,128)S(1)}, u32[]{:S(2)}) copy-start(f32[3,36,32,128]{3,2,1,0:T(8,128)S(1)} %get-tuple-element.13.center) | copy-start | bytes 5308420

commit v2 on v1

v2 whole, which is shorter than its diff:
```python
import functools
import math

import jax
import jax.numpy as jnp
from jax import lax
from jax.experimental import pallas as pl
from jax.experimental.pallas import tpu as pltpu
from jax.sharding import PartitionSpec as P

REACH = 2
NEAR = (-2, -1, 1, 2)
MESH = pl.DeviceIdType.MESH
BF = jnp.bfloat16
F32 = jnp.float32
SIDE_TABLE = (
    ((0, 0), (3, 1), (1, 3), (2, 2)),
    ((1, 0), (2, 1), (0, 3), (3, 2)),
    ((2, 0), (0, 2), (3, 3), (1, 1)),
    ((3, 0), (1, 2), (2, 3), (0, 1)),
)
WANTED = (1, 1, 1, 3, 2, 0, 0, 0)
TORUS = {512: (8, 4, 8), 16: (2, 2, 2)}


def pick(k, values):
    out = jnp.int32(values[3])
    for i in (2, 1, 0):
        out = jnp.where(k == i, jnp.int32(values[i]), out)
    return out


def side_scalars(j, nb, rot, me, count, here):
    owner = nb // here
    off = lax.rem(owner - me + REACH + count, count)
    place = jnp.minimum(off, 2 * REACH) * here + (nb - owner * here)
    table = SIDE_TABLE[WANTED[j]]
    slot = pick(rot, [table[k][0] for k in range(4)])
    c1 = pick(rot, [table[k][1] & 1 for k in range(4)])
    c2 = pick(rot, [table[k][1] >> 1 for k in range(4)])
    return place * 4 + slot, c1, c2


def onehot(target, width):
    rows = target.shape[0]
    lanes = lax.broadcasted_iota(jnp.int32, (rows, width), 1)
    return jnp.where(lanes == target, 1.0, 0.0).astype(BF)


def rows_iota(rows):
    return lax.broadcasted_iota(jnp.int32, (rows, 1), 0)


def flip(c, x, last):
    return last * c + (1 - 2 * c) * x


def dot(a, b):
    return jnp.dot(a, b, preferred_element_type=F32)


def near_kernel(
    count, inp, cot, w, pool, center, zl, zr, wt, cpad, s_edge, r_edge
):
    me = lax.axis_index("patch")
    here = inp.shape[0]
    block = here * 4

    def near(o):
        return lax.rem(me + o + count, count)

    barrier = pltpu.get_barrier_semaphore()
    for o in NEAR:
        pl.semaphore_signal(barrier, inc=1, device_id=(near(o),), device_id_type=MESH)
    r64 = rows_iota(64)
    depth, along = r64 // 32, lax.rem(r64, 32)
    own = REACH * block

    def pack(p, carry):
        pool[own + p * 4] = inp[p, 0:2].reshape(64, 128)
        pool[own + p * 4 + 1] = inp[p, 30:32].reshape(64, 128)
        left = inp[p, :, 0:16, :].reshape(512, 128)
        pool[own + p * 4 + 2] = dot(onehot(along * 16 + depth, 512), left).astype(BF)
        right = inp[p, :, 16:32, :].reshape(512, 128)
        right = dot(onehot(along * 16 + depth + 14, 512), right)
        pool[own + p * 4 + 3] = right.astype(BF)
        return carry

    lax.fori_loop(0, here, pack, 0)
    pl.semaphore_wait(barrier, len(NEAR))
    edges = [
        pltpu.make_async_remote_copy(
            src_ref=pool.at[pl.ds(own, block)],
            dst_ref=pool.at[pl.ds((REACH - o) * block, block)],
            send_sem=s_edge.at[n],
            recv_sem=r_edge.at[n],
            device_id=(near(o),),
            device_id_type=MESH,
        )
        for n, o in enumerate(NEAR)
    ]
    for c in edges:
        c.start()

    for a in range(3):
        for b in range(3):
            piece = w[128 * (3 * a + b) : 128 * (3 * a + b) + 128]
            wt[128 * a : 128 * a + 128, 128 * b : 128 * b + 128] = piece.T
    cpad[0:4] = jnp.zeros((4, 32, 128), BF)
    cpad[36:40] = jnp.zeros((4, 32, 128), BF)
    cols = lax.broadcasted_iota(jnp.int32, (6, 32, 128), 1)

    def patch(p, carry):
        cpad[4:36] = cot[p]

        def chunk(n, c):
            y0 = n * 6
            lhs = jnp.concatenate(
                [cpad[pl.ds(y0 + 4 - 2 * a, 6)].reshape(192, 128) for a in range(3)],
                axis=1,
            )
            z = dot(lhs, wt[...])
            z0 = z[:, 0:128].reshape(6, 32, 128)
            z1 = z[:, 128:256].reshape(6, 32, 128)
            z2 = z[:, 256:384].reshape(6, 32, 128)
            zl[p, pl.ds(y0, 6)] = z0[:, 0:16].astype(BF)
            zr[p, pl.ds(y0, 6)] = z2[:, 16:32].astype(BF)
            total = z1 + jnp.where(cols < 30, pltpu.roll(z0, 30, 1), 0.0)
            total = total + jnp.where(cols >= 2, pltpu.roll(z2, 2, 1), 0.0)
            center[p, pl.ds(y0, 6)] = total
            return c

        lax.fori_loop(0, 6, chunk, 0)
        return carry

    lax.fori_loop(0, here, patch, 0)
    for c in edges:
        c.wait()


def far_kernel(
    sizes,
    factor,
    nb,
    rot,
    cor,
    inp,
    cot,
    w,
    bias,
    pool,
    center,
    zl,
    zr,
    out,
    ingrad,
    fin,
    arr,
    terms,
    tst,
    spots,
    xs,
    cpad,
    wacc,
    wloc,
    core_in,
    p_out,
    p_in,
    z_all,
    s_term,
    r_term,
    s_core,
    r_core,
    s_p,
    r_p,
    s_z,
    r_z,
    s_g,
    r_g,
    s_last,
    r_last,
):
    nz, nx, ny = sizes
    count = nz * nx * ny * 2
    plane = nx * ny
    me = lax.axis_index("patch")
    here = inp.shape[0]
    core = lax.rem(me, 2)
    y = lax.rem(me // 2, ny)
    x = lax.rem(me // (2 * ny), nx)
    z = me // (2 * ny * nx)
    q = x * ny + y
    mate = me + 1 - 2 * core
    block = here * 4
    mr, tr = 1024 // (2 * plane), 128 // (2 * plane)

    def peer_of(k):
        qk = lax.rem(x + k // ny, nx) * ny + lax.rem(y + lax.rem(k, ny), ny)
        return qk, me + 2 * (qk - q)

    def z_peer(k):
        return me + 2 * plane * (lax.rem(z + k, nz) - z)

    def near(o):
        return lax.rem(me + o + count, count)

    def copy(src, dst, send, recv, to):
        return pltpu.make_async_remote_copy(
            src_ref=src,
            dst_ref=dst,
            send_sem=send,
            recv_sem=recv,
            device_id=(to,),
            device_id_type=MESH,
        )

    barrier = pltpu.get_barrier_semaphore()

    def greet(peer):
        pl.semaphore_signal(barrier, inc=1, device_id=(peer,), device_id_type=MESH)

    def greet_plane(k, carry):
        greet(peer_of(k)[1])
        return carry

    for k in range(1, nz):
        greet(z_peer(k))
    lax.fori_loop(1, plane, greet_plane, 0)
    for o in NEAR:
        greet(near(o))
    greet(mate)

    cols = lax.broadcasted_iota(jnp.int32, (32, 32, 128), 1)

    def middle(p, total):
        here_in = inp[p]
        wide = here_in.astype(F32)
        xs[p, 2:34, :, 128:256] = here_in
        ahead = jnp.where(cols >= 2, pltpu.roll(wide, 2, 1), 0.0)
        xs[p, 2:34, :, 0:128] = ahead.astype(BF)
        behind = jnp.where(cols < 30, pltpu.roll(wide, 30, 1), 0.0)
        xs[p, 2:34, :, 256:384] = behind.astype(BF)
        cpad[p, 0:4] = jnp.zeros((4, 32, 128), BF)
        cpad[p, 36:40] = jnp.zeros((4, 32, 128), BF)
        here_cot = cot[p]
        cpad[p, 4:36] = here_cot
        return total + here_cot.astype(F32).reshape(128, 8, 128).sum(axis=0)

    bias8 = lax.fori_loop(0, here, middle, jnp.zeros((8, 128), F32))
    bias_here = jnp.sum(bias8, axis=0, keepdims=True)

    r192 = rows_iota(192)
    which, deep, on = r192 // 64, lax.rem(r192 // 32, 2), lax.rem(r192, 32)
    at = 2 * which + on
    r512 = rows_iota(512)
    line, place = r512 // 16, lax.rem(r512, 16)

    def halo(p, carry):
        def info(j):
            row, c1, c2 = side_scalars(j, nb[p, j], rot[p, j], me, count, here)
            return pool[row], c1, c2, cor[p, j] > 0

        for base, first in ((0, 0), (5, 34)):
            made = jnp.zeros((192, 128), F32)
            for j, c, inside in (
                (base, 30 + at, at < 2),
                (base + 1, at - 2, (at >= 2) & (at < 34)),
                (base + 2, at - 34, at >= 34),
            ):
                strip, c1, c2, present = info(j)
                target = 32 * flip(c1, deep, 1) + flip(c2, c, 31)
                target = jnp.where(inside & present, target, -1)
                made = made + dot(onehot(target, 64), strip)
            made = made.astype(BF)
            for b in range(3):
                piece = made[64 * b : 64 * b + 64].reshape(2, 32, 128)
                xs[p, first : first + 2, :, 128 * b : 128 * b + 128] = piece
        strip, c1, c2, present = info(3)
        target = 32 * flip(c1, place, 1) + flip(c2, line, 31)
        target = jnp.where((place < 2) & present, target, -1)
        made = dot(onehot(target, 64), strip).reshape(32, 16, 128)
        old = xs[p, 2:34, 0:16, 0:128].astype(F32)
        xs[p, 2:34, 0:16, 0:128] = (old + made).astype(BF)
        strip, c1, c2, present = info(4)
        target = 32 * flip(c1, place - 14, 1) + flip(c2, line, 31)
        target = jnp.where((place >= 14) & present, target, -1)
        made = dot(onehot(target, 64), strip).reshape(32, 16, 128)
        old = xs[p, 2:34, 16:32, 256:384].astype(F32)
        xs[p, 2:34, 16:32, 256:384] = (old + made).astype(BF)
        return carry

    lax.fori_loop(0, here, halo, 0)

    wacc[...] = jnp.zeros_like(wacc)

    def outer(n, carry):
        p, y0 = n // 3, lax.rem(n, 3) * 12
        lhs = xs[p, pl.ds(y0, 12)].reshape(384, 384)
        rhs = jnp.concatenate(
            [cpad[p, pl.ds(y0 + 4 - 2 * a, 12)].reshape(384, 128) for a in range(3)],
            axis=1,
        )
        wacc[...] += lax.dot_general(
            lhs, rhs, (((0,), (0,)), ((), ())), preferred_element_type=F32
        )
        return carry

    lax.fori_loop(0, here * 3, outer, 0)

    wide = wloc.shape[1] - mr
    row_t = lax.broadcasted_iota(jnp.int32, (wide, 128), 0)

    def split_bias(tail):
        b = tail[tr : tr + 1] + tail[tr + 1 : tr + 2]
        top = b.astype(BF).astype(F32)
        return jnp.where(row_t == tr, top, jnp.where(row_t == tr + 1, b - top, tail))

    def tap(t):
        a, b = t // 3, t % 3
        return wacc[128 * b : 128 * b + 128, 128 * a : 128 * a + 128]

    each = 128 // mr
    for t in range(8):
        wloc[t * each : (t + 1) * each, 0:mr] = tap(t).reshape(each, mr, 128)
    last = tap(8)
    for s in range(2 * plane):
        rows = [last[s * tr : (s + 1) * tr], bias_here]
        rows.append(jnp.zeros((wide - tr - 1, 128), F32))
        wloc[s, mr:] = jnp.concatenate(rows, axis=0)

    pl.semaphore_wait(barrier, nz - 1 + plane - 1 + len(NEAR) + 1)
    swap = copy(
        wloc.at[pl.ds((1 - core) * plane, plane)], core_in, s_core, r_core, mate
    )
    swap.start()

    def conv(n, carry):
        p, i0 = n // 4, lax.rem(n, 4) * 8
        lhs = jnp.concatenate(
            [xs[p, pl.ds(i0 + 2 * a, 8)].reshape(256, 384) for a in range(3)], axis=1
        )
        out[p, pl.ds(i0, 8)] = (dot(lhs, w[...]) + bias[...]).astype(BF).reshape(8, 32, 128)
        return carry

    lax.fori_loop(0, 2, conv, 0)
    swap.wait_recv()

    def pair(s, carry):
        slab = wloc[core * plane + s] + core_in[s]
        p_out[s, 0:mr] = slab[0:mr].astype(BF)
        p_out[s, mr:] = split_bias(slab[mr:]).astype(BF)
        return carry

    lax.fori_loop(0, plane, pair, 0)

    half = (nx // 2) * ny + ny // 2

    def order(n):
        return lax.rem(n // ny + nx // 2, nx) * ny + lax.rem(lax.rem(n, ny) + ny // 2, ny)

    def p_reduce(k):
        qk, peer = peer_of(k)
        return copy(p_out.at[qk], p_in.at[k - 1], s_p.at[k - 1], r_p.at[k - 1], peer)

    def every(fun, init):
        init = lax.fori_loop(0, half, lambda n, c: fun(order(n), c), init)
        return lax.fori_loop(half + 1, plane, lambda n, c: fun(order(n), c), init)

    def p_start(k, c):
        p_reduce(k).start()
        return c

    every(p_start, 0)

    r64 = rows_iota(64)
    depth, along = r64 // 32, lax.rem(r64, 32)

    def last_two(step, c):
        return jnp.where(c >= 30, step + c - 30, -1)

    def first_two(step, c):
        return jnp.where(c < 2, step + 14 + c, -1)

    def turn_back(p, carry):
        def back(j, target_of, piece):
            row, c1, c2 = side_scalars(j, nb[p, j], rot[p, j], me, count, here)
            target = target_of(flip(c1, depth, 1), flip(c2, along, 31))
            target = jnp.where(cor[p, j] > 0, target, -1)
            spots[p * 8 + j] = row
            tst[p * 8 + j] = dot(onehot(target, piece.shape[0]), piece)

        for base, lo in ((0, 0), (5, 34)):
            mid = center[p, lo : lo + 2].reshape(64, 128).astype(BF)
            ends = zl[p, lo : lo + 2].reshape(32, 128)
            back(base, lambda r, c: last_two(16 * r, c), ends)
            back(base + 1, lambda r, c: 32 * r + c, mid)
            ends = zr[p, lo : lo + 2].reshape(32, 128)
            back(base + 2, lambda r, c: first_two(16 * r, c), ends)
        back(3, lambda c, i: 16 * i + c, zl[p, 2:34].reshape(512, 128))
        back(4, lambda c, i: 16 * i + 14 + c, zr[p, 2:34].reshape(512, 128))
        return carry

    lax.fori_loop(0, here, turn_back, 0)

    def gather_terms(s, carry):
        total = jnp.zeros((64, 128), F32)
        for n in range(here * 8):
            total = total + jnp.where(spots[n] == s, 1.0, 0.0) * tst[n]
        terms[s] = total.astype(BF)
        return carry

    lax.fori_loop(0, 5 * block, gather_terms, 0)
    lax.fori_loop(2, 6, conv, 0)

    def p_add(k, c):
        p_reduce(k).wait_recv()
        return c + p_in[k - 1].astype(F32)

    z_all[z] = every(p_add, wloc[core * plane + q] + core_in[q])

    def z_gather(k):
        return copy(z_all.at[z], z_all.at[z], s_z.at[k - 1], r_z.at[k - 1], z_peer(k))

    for k in range(1, nz):
        z_gather(k).start()
    backs = [
        copy(
            terms.at[pl.ds((REACH + o) * block, block)],
            arr.at[n],
            s_term.at[n],
            r_term.at[n],
            near(o),
        )
        for n, o in enumerate(NEAR)
    ]
    for c in backs:
        c.start()
    lax.fori_loop(6, 4 * here, conv, 0)
    for k in range(1, nz):
        z_gather(k).wait_recv()
    slab = z_all[0]
    for n in range(1, nz):
        slab = slab + z_all[n]
    slab = slab * factor
    spot = core * plane + q
    fin[spot, 0:mr] = slab[0:mr].astype(BF)
    fin[spot, mr:] = split_bias(slab[mr:]).astype(BF)

    def p_gather(k):
        return copy(fin.at[spot], fin.at[spot], s_g.at[k - 1], r_g.at[k - 1], peer_of(k)[1])

    def g_start(k, c):
        p_gather(k).start()
        return c

    every(g_start, 0)
    for c in backs:
        c.wait_recv()

    def finish(p, carry):
        def pieces_of(slot):
            found = [terms[REACH * block + p * 4 + slot]]
            return found + [arr[n, p * 4 + slot] for n in range(len(NEAR))]

        def arrived(slot):
            total = jnp.zeros((64, 128), F32)
            for piece in pieces_of(slot):
                total = total + piece.astype(F32)
            return total.reshape(2, 32, 128)

        top, bottom = arrived(0), arrived(1)
        for slot, shift, lo in ((2, 0, 0), (3, 14, 16)):
            at_col = place - shift
            inside = (at_col >= 0) & (at_col < 2)
            spread = onehot(jnp.where(inside, 32 * at_col + line, -1), 64)
            made = jnp.zeros((512, 128), F32)
            for piece in pieces_of(slot):
                made = made + dot(spread, piece)
            total = center[p, 2:34, lo : lo + 16] + made.reshape(32, 16, 128)
            upper = total[0:2] + top[:, lo : lo + 16]
            lower = total[30:32] + bottom[:, lo : lo + 16]
            ingrad[p, 0:2, lo : lo + 16] = upper.astype(BF)
            ingrad[p, 2:30, lo : lo + 16] = total[2:30].astype(BF)
            ingrad[p, 30:32, lo : lo + 16] = lower.astype(BF)
        return carry

    lax.fori_loop(0, here, finish, 0)

    def g_wait(k, c):
        p_gather(k).wait_recv()
        return c

    every(g_wait, 0)
    mine = fin.at[pl.ds(core * plane, plane)]
    hand = copy(mine, mine, s_last, r_last, mate)
    hand.start()

    def sent(k, c):
        p_reduce(k).wait_send()
        p_gather(k).wait_send()
        return c

    every(sent, 0)
    for c in backs + [swap]:
        c.wait_send()
    for k in range(1, nz):
        z_gather(k).wait_send()
    hand.wait()


def body(count, inputs, cotangent, weights, bias_vector, neighbours, rotations, corners):
    here, length, _, chans = inputs.shape
    sizes = TORUS[count]
    nz, nx, ny = sizes
    plane = nx * ny
    factor = 1.0 / (length * math.sqrt(here * count))
    block = here * 4
    smem = pl.BlockSpec(memory_space=pltpu.SMEM)
    vmem = pl.BlockSpec(memory_space=pltpu.VMEM)
    dma = pltpu.SemaphoreType.DMA
    flat = weights.reshape(9 * chans, chans)
    pool, center, zl, zr = pl.pallas_call(
        functools.partial(near_kernel, count),
        out_shape=(
            jax.ShapeDtypeStruct((5 * block, 64, chans), BF),
            jax.ShapeDtypeStruct((here, 36, 32, chans), F32),
            jax.ShapeDtypeStruct((here, 36, 16, chans), BF),
            jax.ShapeDtypeStruct((here, 36, 16, chans), BF),
        ),
        in_specs=[vmem] * 3,
        out_specs=(vmem,) * 4,
        scratch_shapes=[
            pltpu.VMEM((3 * chans, 3 * chans), BF),
            pltpu.VMEM((40, 32, chans), BF),
            dma((len(NEAR),)),
            dma((len(NEAR),)),
        ],
        compiler_params=pltpu.CompilerParams(
            collective_id=1, has_side_effects=True, vmem_limit_bytes=16 * 2**20
        ),
    )(inputs, cotangent, flat)

    mr, tr = 1024 // (2 * plane), 128 // (2 * plane)
    rows = mr + -(-(tr + 2) // 8) * 8
    outputs, input_grad, fin = pl.pallas_call(
        functools.partial(far_kernel, sizes, factor),
        out_shape=(
            jax.ShapeDtypeStruct(inputs.shape, BF),
            jax.ShapeDtypeStruct(inputs.shape, BF),
            jax.ShapeDtypeStruct((2 * plane, rows, chans), BF),
        ),
        in_specs=[smem] * 3 + [vmem] * 8,
        out_specs=(vmem,) * 3,
        scratch_shapes=[
            pltpu.VMEM((len(NEAR), block, 64, chans), BF),
            pltpu.VMEM((5 * block, 64, chans), BF),
            pltpu.VMEM((here * 8, 64, chans), F32),
            pltpu.SMEM((here * 8,), jnp.int32),
            pltpu.VMEM((here, 36, 32, 3 * chans), BF),
            pltpu.VMEM((here, 40, 32, chans), BF),
            pltpu.VMEM((3 * chans, 3 * chans), F32),
            pltpu.VMEM((2 * plane, rows, chans), F32),
            pltpu.VMEM((plane, rows, chans), F32),
            pltpu.VMEM((plane, rows, chans), BF),
            pltpu.VMEM((plane - 1, rows, chans), BF),
            pltpu.VMEM((nz, rows, chans), F32),
            dma((len(NEAR),)),
            dma((len(NEAR),)),
            dma,
            dma,
            dma((plane - 1,)),
            dma((plane - 1,)),
            dma((nz - 1,)),
            dma((nz - 1,)),
            dma((plane - 1,)),
            dma((plane - 1,)),
            dma,
            dma,
        ],
        compiler_params=pltpu.CompilerParams(
            collective_id=0, has_side_effects=True, vmem_limit_bytes=26 * 2**20
        ),
    )(
        neighbours,
        rotations,
        corners,
        inputs,
        cotangent,
        flat,
        bias_vector.reshape(1, chans),
        pool,
        center,
        zl,
        zr,
    )
    main = fin[:, 0:mr].reshape(8 * chans, chans)
    rest = fin[:, mr : mr + tr].reshape(chans, chans)
    weight_grad = jnp.concatenate([main, rest], axis=0).astype(F32)
    bias_grad = fin[0, mr + tr].astype(F32) + fin[0, mr + tr + 1].astype(F32)
    return (outputs, input_grad, weight_grad.reshape(weights.shape), bias_grad)


def solution(mesh):
    in_specs = (
        P("patch", None, None, None),
        P("patch", None, None, None),
        P(),
        P(),
        P("patch", None),
        P("patch", None),
        P("patch", None),
    )
    out_specs = (P("patch", None, None, None), P("patch", None, None, None), P(), P())
    return jax.shard_map(
        functools.partial(body, mesh.shape["patch"]),
        mesh=mesh,
        in_specs=in_specs,
        out_specs=out_specs,
        check_vma=False,
    )
```

time: 76.8 us -> 69.4 us (0.904)
  Pallas kernels: 66.9 us -> 61.9 us
  local copies, waits for them, and re-layouts: 8.85 us -> 5.06 us
  other arithmetic: 0 us -> 1.4 us
    pallas_call x2, Pallas kernels: 66.9 us -> 61.9 us  [the longest x1 37.9 us: body(): pl.pallas_call(functools.partial(far_kernel, sizes, factor), out_shape=(j...]
    unnamed x28 -> x22, local copies, waits for them, and re-layouts: 7.05 us -> 5.02 us
    transpose x1 -> x0, local copies, waits for them, and re-layouts: 1.29 us -> none  [body(): turned = weights.transpose(0, 3, 1, 2).reshape(3 * chans, 3 * chans)]
    convert_element_type x0 -> x1, other arithmetic: none -> 0.86 us  [body(): weight_grad = jnp.concatenate([main, rest], axis=0).astype(F32)]
where the time goes in v2:
time: 69.4 us; the launch traced here: 69.1 us
  Pallas kernels  61.9 us (89%)
  local copies, waits for them, and re-layouts  5.06 us (7%)
  other arithmetic  1.4 us (2%)
  between operations  0.76 us (1%)
    pallas_call x1, Pallas kernels, body(): pl.pallas_call(functools.partial(far_kernel, sizes, factor), out_shape=(j...  37.9 us
    pallas_call x1, Pallas kernels, body(): pl.pallas_call(functools.partial(near_kernel, count), out_shape=(jax.Shap...  24 us
    unnamed x22, local copies, waits for them, and re-layouts  5.02 us

profile of v2, /device:TPU:1, one launch (start us, length us, event | category | flops | bytes accessed | tf_op | source)
XLA Modules:
  0.0 69.1 jit_solution(13837394983605746244)
XLA Ops:
  0.6 0.0 copy-start.6
  0.6 0.0 copy-start.9
  0.7 0.0 copy-start
  0.7 1.1 %copy-done = bf16[3,32,32,128]{3,2,1,0:T(8,128)(2,1)S(1)} copy-done((bf16[3,32,32,128]{3,2,1,0:T(8,128)(2,1)S(1)}, bf16[3,32,32,128]{3,2,1,0:T(8,128)(2,1)}, u32[]{:S(2)}) %copy-start) | copy-done | bytes 786456
  1.8 0.0 copy-start.2
  1.8 1.1 %copy-done.2 = bf16[3,32,32,128]{3,2,1,0:T(8,128)(2,1)S(1)} copy-done((bf16[3,32,32,128]{3,2,1,0:T(8,128)(2,1)S(1)}, bf16[3,32,32,128]{3,2,1,0:T(8,128)(2,1)}, u32[]{:S(2)}) %copy-start.2) | copy-done | bytes 786456
  2.9 0.0 copy-start.4
  2.9 1.0 %copy-done.4 = bf16[3,3,128,128]{3,2,1,0:T(8,128)(2,1)S(1)} copy-done((bf16[3,3,128,128]{3,2,1,0:T(8,128)(2,1)S(1)}, bf16[3,3,128,128]{3,2,1,0:T(8,128)(2,1)}, u32[]{:S(2)}) %copy-start.4) | copy-done | bytes 294936
  3.9 0.0 copy-start.1
  3.9 0.0 copy-start.3
  3.9 0.0 copy-start.5
  3.9 0.0 copy-start.7
  3.9 0.0 copy-start.8
  3.9 24.0 %shard_map.102 = (bf16[60,64,128]{2,1,0:T(8,128)(2,1)S(1)}, f32[3,36,32,128]{3,2,1,0:T(8,128)S(1)}, bf16[3,36,16,128]{3,2,1,0:T(8,128)(2,1)S(1)}, bf16[3,36,16,128]{3,2,1,0:T(8,128)(2,1)S(1)}) custom-call(bf16[3,32,32,128]{3,2,1,0:T(8,128)(2,1)S(1)} %copy-done, bf16[3,32,32,128]{3,2,1,0:T(8,128)(2,1)S(1)} %copy-done.2, bf16[1152,128]{1,0:T(8,128)(2,1)S(1)} %bitcast.8), custom_call_target="tpu_custom_call" | custom-call | tf_op jit(solution)/shard_map/pallas_call | solution.py:522
  27.9 0.0 copy-done.6
  27.9 0.0 copy-done.9
  27.9 0.0 copy-done.1
  27.9 0.0 copy-done.3
  27.9 0.0 copy-done.5
  28.0 0.0 copy-done.7
  28.0 0.0 copy-done.8
  28.0 37.9 %shard_map.103 = (bf16[3,32,32,128]{3,2,1,0:T(8,128)(2,1)S(1)}, bf16[3,32,32,128]{3,2,1,0:T(8,128)(2,1)S(1)}, bf16[64,24,128]{2,1,0:T(8,128)(2,1)S(1)}) custom-call(s32[3,8]{1,0:T(4,128)S(1)} %copy-done.6, s32[3,8]{1,0:T(4,128)S(1)} %copy-done.7, s32[3,8]{1,0:T(4,128)S(1)} %copy-done.8, bf16[3,32,32,128]{3,2,1,0:T(8,128)(2,1)S(1)} %copy-done.1, ...), custom_call_target="tpu_custom_call" | custom-call | tf_op jit(solution)/shard_map/pallas_call | solution.py:545
  65.9 0.5 add_bitcast_fusion
  66.5 0.9 %convert.1 = f32[3,3,128,128]{3,2,1,0:T(8,128)} convert(bf16[3,3,128,128]{3,2,1,0:T(8,128)(2,1)S(1)} %bitcast.11) | non-fusion elementwise | flops 147456 | bytes 884736 | tf_op jit(solution)/shard_map/convert_element_type | solution.py:598
  67.4 0.9 %copy.13 = bf16[3,32,32,128]{3,2,1,0:T(8,128)(2,1)} copy(bf16[3,32,32,128]{3,2,1,0:T(8,128)(2,1)S(1)} %get-tuple-element.22) | data formatting | bytes 1572864
  68.3 0.9 %copy.14 = bf16[3,32,32,128]{3,2,1,0:T(8,128)(2,1)} copy(bf16[3,32,32,128]{3,2,1,0:T(8,128)(2,1)S(1)} %get-tuple-element.23) | data formatting | bytes 1572864
  (3 shorter events, 0.1 us)
Async XLA Ops:
  0.6 27.3 %copy-start.6 = (s32[3,8]{1,0:T(4,128)S(1)}, s32[3,8]{1,0:T(4,128)}, u32[]{:S(2)}) copy-start(s32[3,8]{1,0:T(4,128)} %nb.1) | copy-start | bytes 292
  0.6 27.3 %copy-start.9 = (f32[128]{0:T(128)S(1)}, f32[128]{0:T(128)}, u32[]{:S(2)}) copy-start(f32[128]{0:T(128)} %param.10) | copy-start | bytes 1540
  0.7 1.1 %copy-start = (bf16[3,32,32,128]{3,2,1,0:T(8,128)(2,1)S(1)}, bf16[3,32,32,128]{3,2,1,0:T(8,128)(2,1)}, u32[]{:S(2)}) copy-start(bf16[3,32,32,128]{3,2,1,0:T(8,128)(2,1)} %inp.3) | copy-start | bytes 2359300
  1.8 1.1 %copy-start.2 = (bf16[3,32,32,128]{3,2,1,0:T(8,128)(2,1)S(1)}, bf16[3,32,32,128]{3,2,1,0:T(8,128)(2,1)}, u32[]{:S(2)}) copy-start(bf16[3,32,32,128]{3,2,1,0:T(8,128)(2,1)} %cot.3) | copy-start | bytes 2359300
  2.9 1.0 %copy-start.4 = (bf16[3,3,128,128]{3,2,1,0:T(8,128)(2,1)S(1)}, bf16[3,3,128,128]{3,2,1,0:T(8,128)(2,1)}, u32[]{:S(2)}) copy-start(bf16[3,3,128,128]{3,2,1,0:T(8,128)(2,1)} %param.9) | copy-start | bytes 884740
  3.9 24.0 %copy-start.1 = (bf16[3,32,32,128]{3,2,1,0:T(8,128)(2,1)S(1)}, bf16[3,32,32,128]{3,2,1,0:T(8,128)(2,1)}, u32[]{:S(2)}) copy-start(bf16[3,32,32,128]{3,2,1,0:T(8,128)(2,1)} %inp.3) | copy-start | bytes 2359300
  3.9 24.0 %copy-start.3 = (bf16[3,32,32,128]{3,2,1,0:T(8,128)(2,1)S(1)}, bf16[3,32,32,128]{3,2,1,0:T(8,128)(2,1)}, u32[]{:S(2)}) copy-start(bf16[3,32,32,128]{3,2,1,0:T(8,128)(2,1)} %cot.3) | copy-start | bytes 2359300
  3.9 24.1 %copy-start.5 = (bf16[3,3,128,128]{3,2,1,0:T(8,128)(2,1)S(1)}, bf16[3,3,128,128]{3,2,1,0:T(8,128)(2,1)}, u32[]{:S(2)}) copy-start(bf16[3,3,128,128]{3,2,1,0:T(8,128)(2,1)} %param.9) | copy-start | bytes 884740
  3.9 24.1 %copy-start.7 = (s32[3,8]{1,0:T(4,128)S(1)}, s32[3,8]{1,0:T(4,128)}, u32[]{:S(2)}) copy-start(s32[3,8]{1,0:T(4,128)} %rot.1) | copy-start | bytes 292
  3.9 24.1 %copy-start.8 = (s32[3,8]{1,0:T(4,128)S(1)}, s32[3,8]{1,0:T(4,128)}, u32[]{:S(2)}) copy-start(s32[3,8]{1,0:T(4,128)} %cor.1) | copy-start | bytes 292

commit v3 on v2

--- a/solution.py
+++ b/solution.py
@@ -59,102 +59,33 @@
     return jnp.dot(a, b, preferred_element_type=F32)
 
 
-def near_kernel(
-    count, inp, cot, w, pool, center, zl, zr, wt, cpad, s_edge, r_edge
-):
-    me = lax.axis_index("patch")
-    here = inp.shape[0]
-    block = here * 4
-
-    def near(o):
-        return lax.rem(me + o + count, count)
-
-    barrier = pltpu.get_barrier_semaphore()
-    for o in NEAR:
-        pl.semaphore_signal(barrier, inc=1, device_id=(near(o),), device_id_type=MESH)
-    r64 = rows_iota(64)
-    depth, along = r64 // 32, lax.rem(r64, 32)
-    own = REACH * block
-
-    def pack(p, carry):
-        pool[own + p * 4] = inp[p, 0:2].reshape(64, 128)
-        pool[own + p * 4 + 1] = inp[p, 30:32].reshape(64, 128)
-        left = inp[p, :, 0:16, :].reshape(512, 128)
-        pool[own + p * 4 + 2] = dot(onehot(along * 16 + depth, 512), left).astype(BF)
-        right = inp[p, :, 16:32, :].reshape(512, 128)
-        right = dot(onehot(along * 16 + depth + 14, 512), right)
-        pool[own + p * 4 + 3] = right.astype(BF)
-        return carry
-
-    lax.fori_loop(0, here, pack, 0)
-    pl.semaphore_wait(barrier, len(NEAR))
-    edges = [
-        pltpu.make_async_remote_copy(
-            src_ref=pool.at[pl.ds(own, block)],
-            dst_ref=pool.at[pl.ds((REACH - o) * block, block)],
-            send_sem=s_edge.at[n],
-            recv_sem=r_edge.at[n],
-            device_id=(near(o),),
-            device_id_type=MESH,
-        )
-        for n, o in enumerate(NEAR)
-    ]
-    for c in edges:
-        c.start()
-
-    for a in range(3):
-        for b in range(3):
-            piece = w[128 * (3 * a + b) : 128 * (3 * a + b) + 128]
-            wt[128 * a : 128 * a + 128, 128 * b : 128 * b + 128] = piece.T
-    cpad[0:4] = jnp.zeros((4, 32, 128), BF)
-    cpad[36:40] = jnp.zeros((4, 32, 128), BF)
-    cols = lax.broadcasted_iota(jnp.int32, (6, 32, 128), 1)
-
-    def patch(p, carry):
-        cpad[4:36] = cot[p]
-
-        def chunk(n, c):
-            y0 = n * 6
-            lhs = jnp.concatenate(
-                [cpad[pl.ds(y0 + 4 - 2 * a, 6)].reshape(192, 128) for a in range(3)],
-                axis=1,
-            )
-            z = dot(lhs, wt[...])
-            z0 = z[:, 0:128].reshape(6, 32, 128)
-            z1 = z[:, 128:256].reshape(6, 32, 128)
-            z2 = z[:, 256:384].reshape(6, 32, 128)
-            zl[p, pl.ds(y0, 6)] = z0[:, 0:16].astype(BF)
-            zr[p, pl.ds(y0, 6)] = z2[:, 16:32].astype(BF)
-            total = z1 + jnp.where(cols < 30, pltpu.roll(z0, 30, 1), 0.0)
-            total = total + jnp.where(cols >= 2, pltpu.roll(z2, 2, 1), 0.0)
-            center[p, pl.ds(y0, 6)] = total
-            return c
-
-        lax.fori_loop(0, 6, chunk, 0)
-        return carry
-
-    lax.fori_loop(0, here, patch, 0)
-    for c in edges:
-        c.wait()
-
-
-def far_kernel(
+def main_kernel(
     sizes,
     factor,
+    nb_in,
+    rot_in,
+    cor_in,
+    inp_in,
+    cot_in,
+    w_in,
+    bias_in,
+    out_o,
+    ingrad_o,
+    fin_o,
+    out,
+    ingrad,
+    fin,
     nb,
     rot,
     cor,
     inp,
-    cot,
     w,
     bias,
+    wt,
     pool,
     center,
     zl,
     zr,
-    out,
-    ingrad,
-    fin,
     arr,
     terms,
     tst,
@@ -167,6 +98,10 @@
     p_out,
     p_in,
     z_all,
+    s_load,
+    s_store,
+    s_edge,
+    r_edge,
     s_term,
     r_term,
     s_core,
@@ -185,6 +120,16 @@
     plane = nx * ny
     me = lax.axis_index("patch")
     here = inp.shape[0]
+    loads = [
+        pltpu.make_async_copy(src, dst, s_load.at[n])
+        for n, (src, dst) in enumerate(
+            [(inp_in, inp), (nb_in, nb), (rot_in, rot), (cor_in, cor)]
+            + [(w_in, w), (bias_in, bias)]
+            + [(cot_in.at[p], cpad.at[p, 4:36]) for p in range(here)]
+        )
+    ]
+    for c in loads:
+        c.start()
     core = lax.rem(me, 2)
     y = lax.rem(me // 2, ny)
     x = lax.rem(me // (2 * ny), nx)
@@ -229,6 +174,38 @@
     for o in NEAR:
         greet(near(o))
     greet(mate)
+
+    r64 = rows_iota(64)
+    depth, along = r64 // 32, lax.rem(r64, 32)
+    own = REACH * block
+    loads[0].wait()
+
+    def pack(p, carry):
+        pool[own + p * 4] = inp[p, 0:2].reshape(64, 128)
+        pool[own + p * 4 + 1] = inp[p, 30:32].reshape(64, 128)
+        left = inp[p, :, 0:16, :].reshape(512, 128)
+        pool[own + p * 4 + 2] = dot(onehot(along * 16 + depth, 512), left).astype(BF)
+        right = inp[p, :, 16:32, :].reshape(512, 128)
+        right = dot(onehot(along * 16 + depth + 14, 512), right)
+        pool[own + p * 4 + 3] = right.astype(BF)
+        return carry
+
+    lax.fori_loop(0, here, pack, 0)
+    pl.semaphore_wait(barrier, nz - 1 + plane - 1 + len(NEAR) + 1)
+    edges = [
+        copy(
+            pool.at[pl.ds(own, block)],
+            pool.at[pl.ds((REACH - o) * block, block)],
+            s_edge.at[n],
+            r_edge.at[n],
+            near(o),
+        )
+        for n, o in enumerate(NEAR)
+    ]
+    for c in edges:
+        c.start()
+    for c in loads[1:]:
+        c.wait()
 
     cols = lax.broadcasted_iota(jnp.int32, (32, 32, 128), 1)
 
@@ -242,12 +219,56 @@
         xs[p, 2:34, :, 256:384] = behind.astype(BF)
         cpad[p, 0:4] = jnp.zeros((4, 32, 128), BF)
         cpad[p, 36:40] = jnp.zeros((4, 32, 128), BF)
-        here_cot = cot[p]
-        cpad[p, 4:36] = here_cot
+        here_cot = cpad[p, 4:36]
         return total + here_cot.astype(F32).reshape(128, 8, 128).sum(axis=0)
 
     bias8 = lax.fori_loop(0, here, middle, jnp.zeros((8, 128), F32))
     bias_here = jnp.sum(bias8, axis=0, keepdims=True)
+    wacc[...] = jnp.zeros_like(wacc)
+
+    def outer_dot(a, b):
+        return lax.dot_general(
+            a, b, (((0,), (0,)), ((), ())), preferred_element_type=F32
+        )
+
+    def inner(n, carry):
+        p, y0 = n // 4, lax.rem(n, 4) * 8 + 2
+        lhs = xs[p, pl.ds(y0, 8)].reshape(256, 384)
+        rhs = jnp.concatenate(
+            [cpad[p, pl.ds(y0 + 4 - 2 * a, 8)].reshape(256, 128) for a in range(3)],
+            axis=1,
+        )
+        wacc[...] += outer_dot(lhs, rhs)
+        return carry
+
+    lax.fori_loop(0, here * 4, inner, 0)
+
+    for a in range(3):
+        for b in range(3):
+            piece = w[128 * (3 * a + b) : 128 * (3 * a + b) + 128]
+            wt[128 * a : 128 * a + 128, 128 * b : 128 * b + 128] = piece.T
+    cols6 = lax.broadcasted_iota(jnp.int32, (6, 32, 128), 1)
+
+    def spread_back(n, carry):
+        p, y0 = n // 6, lax.rem(n, 6) * 6
+        lhs = jnp.concatenate(
+            [cpad[p, pl.ds(y0 + 4 - 2 * a, 6)].reshape(192, 128) for a in range(3)],
+            axis=1,
+        )
+        got = dot(lhs, wt[...])
+        z0 = got[:, 0:128].reshape(6, 32, 128)
+        z1 = got[:, 128:256].reshape(6, 32, 128)
+        z2 = got[:, 256:384].reshape(6, 32, 128)
+        zl[p, pl.ds(y0, 6)] = z0[:, 0:16].astype(BF)
+        zr[p, pl.ds(y0, 6)] = z2[:, 16:32].astype(BF)
+        total = z1 + jnp.where(cols6 < 30, pltpu.roll(z0, 30, 1), 0.0)
+        total = total + jnp.where(cols6 >= 2, pltpu.roll(z2, 2, 1), 0.0)
+        center[p, pl.ds(y0, 6)] = total
+        return carry
+
+    lax.fori_loop(0, here * 3, spread_back, 0)
+    for c in edges:
+        c.wait_recv()
 
     r192 = rows_iota(192)
     which, deep, on = r192 // 64, lax.rem(r192 // 32, 2), lax.rem(r192, 32)
@@ -275,37 +296,33 @@
             for b in range(3):
                 piece = made[64 * b : 64 * b + 64].reshape(2, 32, 128)
                 xs[p, first : first + 2, :, 128 * b : 128 * b + 128] = piece
-        strip, c1, c2, present = info(3)
-        target = 32 * flip(c1, place, 1) + flip(c2, line, 31)
-        target = jnp.where((place < 2) & present, target, -1)
-        made = dot(onehot(target, 64), strip).reshape(32, 16, 128)
-        old = xs[p, 2:34, 0:16, 0:128].astype(F32)
-        xs[p, 2:34, 0:16, 0:128] = (old + made).astype(BF)
-        strip, c1, c2, present = info(4)
-        target = 32 * flip(c1, place - 14, 1) + flip(c2, line, 31)
-        target = jnp.where((place >= 14) & present, target, -1)
-        made = dot(onehot(target, 64), strip).reshape(32, 16, 128)
-        old = xs[p, 2:34, 16:32, 256:384].astype(F32)
-        xs[p, 2:34, 16:32, 256:384] = (old + made).astype(BF)
+        wacc[:, 0:128] += outer_dot(
+            xs[p, 0:2].reshape(64, 384), cpad[p, 4:6].reshape(64, 128)
+        )
+        wacc[:, 256:384] += outer_dot(
+            xs[p, 34:36].reshape(64, 384), cpad[p, 34:36].reshape(64, 128)
+        )
+        for j, shift, lo, lane in ((3, 0, 0, 0), (4, 14, 16, 256)):
+            strip, c1, c2, present = info(j)
+            side = place - shift
+            target = 32 * flip(c1, side, 1) + flip(c2, line, 31)
+            inside = (side >= 0) & (side < 2) & present
+            made = dot(onehot(jnp.where(inside, target, -1), 64), strip)
+            rhs = jnp.concatenate(
+                [
+                    cpad[p, 6 - 2 * a : 38 - 2 * a, lo : lo + 16].reshape(512, 128)
+                    for a in range(3)
+                ],
+                axis=1,
+            )
+            wacc[lane : lane + 128] += outer_dot(made.astype(BF), rhs)
+            old = xs[p, 2:34, lo : lo + 16, lane : lane + 128].astype(F32)
+            xs[p, 2:34, lo : lo + 16, lane : lane + 128] = (
+                old + made.reshape(32, 16, 128)
+            ).astype(BF)
         return carry
 
     lax.fori_loop(0, here, halo, 0)
-
-    wacc[...] = jnp.zeros_like(wacc)
-
-    def outer(n, carry):
-        p, y0 = n // 3, lax.rem(n, 3) * 12
-        lhs = xs[p, pl.ds(y0, 12)].reshape(384, 384)
-        rhs = jnp.concatenate(
-            [cpad[p, pl.ds(y0 + 4 - 2 * a, 12)].reshape(384, 128) for a in range(3)],
-            axis=1,
-        )
-        wacc[...] += lax.dot_general(
-            lhs, rhs, (((0,), (0,)), ((), ())), preferred_element_type=F32
-        )
-        return carry
-
-    lax.fori_loop(0, here * 3, outer, 0)
 
     wide = wloc.shape[1] - mr
     row_t = lax.broadcasted_iota(jnp.int32, (wide, 128), 0)
@@ -328,7 +345,6 @@
         rows.append(jnp.zeros((wide - tr - 1, 128), F32))
         wloc[s, mr:] = jnp.concatenate(rows, axis=0)
 
-    pl.semaphore_wait(barrier, nz - 1 + plane - 1 + len(NEAR) + 1)
     swap = copy(
         wloc.at[pl.ds((1 - core) * plane, plane)], core_in, s_core, r_core, mate
     )
@@ -342,16 +358,8 @@
         out[p, pl.ds(i0, 8)] = (dot(lhs, w[...]) + bias[...]).astype(BF).reshape(8, 32, 128)
         return carry
 
-    lax.fori_loop(0, 2, conv, 0)
+    lax.fori_loop(here * 3, here * 4, spread_back, 0)
     swap.wait_recv()
-
-    def pair(s, carry):
-        slab = wloc[core * plane + s] + core_in[s]
-        p_out[s, 0:mr] = slab[0:mr].astype(BF)
-        p_out[s, mr:] = split_bias(slab[mr:]).astype(BF)
-        return carry
-
-    lax.fori_loop(0, plane, pair, 0)
 
     half = (nx // 2) * ny + ny // 2
 
@@ -367,13 +375,15 @@
         return lax.fori_loop(half + 1, plane, lambda n, c: fun(order(n), c), init)
 
     def p_start(k, c):
+        qk = peer_of(k)[0]
+        slab = wloc[core * plane + qk] + core_in[qk]
+        p_out[qk, 0:mr] = slab[0:mr].astype(BF)
+        p_out[qk, mr:] = split_bias(slab[mr:]).astype(BF)
         p_reduce(k).start()
         return c
 
     every(p_start, 0)
-
-    r64 = rows_iota(64)
-    depth, along = r64 // 32, lax.rem(r64, 32)
+    lax.fori_loop(here * 4, here * 6, spread_back, 0)
 
     def last_two(step, c):
         return jnp.where(c >= 30, step + c - 30, -1)
@@ -400,8 +410,6 @@
         back(4, lambda c, i: 16 * i + 14 + c, zr[p, 2:34].reshape(512, 128))
         return carry
 
-    lax.fori_loop(0, here, turn_back, 0)
-
     def gather_terms(s, carry):
         total = jnp.zeros((64, 128), F32)
         for n in range(here * 8):
@@ -409,8 +417,8 @@
         terms[s] = total.astype(BF)
         return carry
 
+    lax.fori_loop(0, here, turn_back, 0)
     lax.fori_loop(0, 5 * block, gather_terms, 0)
-    lax.fori_loop(2, 6, conv, 0)
 
     def p_add(k, c):
         p_reduce(k).wait_recv()
@@ -435,7 +443,10 @@
     ]
     for c in backs:
         c.start()
-    lax.fori_loop(6, 4 * here, conv, 0)
+
+    lax.fori_loop(0, 4 * here, conv, 0)
+    stores = [pltpu.make_async_copy(out, out_o, s_store.at[0])]
+    stores[0].start()
     for k in range(1, nz):
         z_gather(k).wait_recv()
     slab = z_all[0]
@@ -485,15 +496,19 @@
         return carry
 
     lax.fori_loop(0, here, finish, 0)
+    stores.append(pltpu.make_async_copy(ingrad, ingrad_o, s_store.at[1]))
+    stores[1].start()
 
     def g_wait(k, c):
         p_gather(k).wait_recv()
         return c
 
     every(g_wait, 0)
-    mine = fin.at[pl.ds(core * plane, plane)]
-    hand = copy(mine, mine, s_last, r_last, mate)
+    mine = pl.ds(core * plane, plane)
+    hand = copy(fin.at[mine], fin_o.at[mine], s_last, r_last, mate)
     hand.start()
+    stores.append(pltpu.make_async_copy(fin.at[mine], fin_o.at[mine], s_store.at[2]))
+    stores[2].start()
 
     def sent(k, c):
         p_reduce(k).wait_send()
@@ -501,11 +516,40 @@
         return c
 
     every(sent, 0)
-    for c in backs + [swap]:
+    for c in edges + backs + [swap]:
         c.wait_send()
     for k in range(1, nz):
         z_gather(k).wait_send()
+    for c in stores:
+        c.wait()
     hand.wait()
+
+
+def write_kernel(
+    mr, tr, out, ingrad, fin_o, out_o, ingrad_o, wgrad_o, bgrad, fin, wide, sems
+):
+    here = out.shape[0]
+    load = pltpu.make_async_copy(fin_o, fin, sems.at[0])
+    load.start()
+    moves = []
+    for p in range(here):
+        for n, (src, dst) in enumerate(((out, out_o), (ingrad, ingrad_o))):
+            moves.append(
+                pltpu.make_async_copy(src.at[p], dst.at[p], sems.at[2 + 2 * p + n])
+            )
+            moves[-1].start()
+    load.wait()
+    slabs = fin.shape[0]
+    wide[0:1024] = fin[:, 0:mr].astype(F32).reshape(1024, 128)
+    for s in range(slabs):
+        tail = fin[s, mr:].astype(F32)
+        wide[1024 + tr * s : 1024 + tr * (s + 1)] = tail[0:tr]
+    moves.append(pltpu.make_async_copy(wide, wgrad_o, sems.at[1]))
+    moves[-1].start()
+    tail = fin[0, mr:].astype(F32)
+    bgrad[...] = tail[tr : tr + 1] + tail[tr + 1 : tr + 2]
+    for c in moves:
+        c.wait()
 
 
 def body(count, inputs, cotangent, weights, bias_vector, neighbours, rotations, corners):
@@ -515,44 +559,38 @@
     plane = nx * ny
     factor = 1.0 / (length * math.sqrt(here * count))
     block = here * 4
-    smem = pl.BlockSpec(memory_space=pltpu.SMEM)
+    hbm = pl.BlockSpec(memory_space=pltpu.HBM)
     vmem = pl.BlockSpec(memory_space=pltpu.VMEM)
     dma = pltpu.SemaphoreType.DMA
-    flat = weights.reshape(9 * chans, chans)
-    pool, center, zl, zr = pl.pallas_call(
-        functools.partial(near_kernel, count),
-        out_shape=(
-            jax.ShapeDtypeStruct((5 * block, 64, chans), BF),
-            jax.ShapeDtypeStruct((here, 36, 32, chans), F32),
-            jax.ShapeDtypeStruct((here, 36, 16, chans), BF),
-            jax.ShapeDtypeStruct((here, 36, 16, chans), BF),
-        ),
-        in_specs=[vmem] * 3,
-        out_specs=(vmem,) * 4,
-        scratch_shapes=[
-            pltpu.VMEM((3 * chans, 3 * chans), BF),
-            pltpu.VMEM((40, 32, chans), BF),
-            dma((len(NEAR),)),
-            dma((len(NEAR),)),
-        ],
-        compiler_params=pltpu.CompilerParams(
-            collective_id=1, has_side_effects=True, vmem_limit_bytes=16 * 2**20
-        ),
-    )(inputs, cotangent, flat)
-
     mr, tr = 1024 // (2 * plane), 128 // (2 * plane)
     rows = mr + -(-(tr + 2) // 8) * 8
+    near = len(NEAR)
+    wires = [near, near, None, plane - 1, nz - 1, plane - 1, None]
     outputs, input_grad, fin = pl.pallas_call(
-        functools.partial(far_kernel, sizes, factor),
+        functools.partial(main_kernel, sizes, factor),
         out_shape=(
             jax.ShapeDtypeStruct(inputs.shape, BF),
             jax.ShapeDtypeStruct(inputs.shape, BF),
             jax.ShapeDtypeStruct((2 * plane, rows, chans), BF),
         ),
-        in_specs=[smem] * 3 + [vmem] * 8,
-        out_specs=(vmem,) * 3,
+        in_specs=[hbm] * 7,
+        out_specs=(hbm,) * 3,
         scratch_shapes=[
-            pltpu.VMEM((len(NEAR), block, 64, chans), BF),
+            pltpu.VMEM(inputs.shape, BF),
+            pltpu.VMEM(inputs.shape, BF),
+            pltpu.VMEM((2 * plane, rows, chans), BF),
+            pltpu.SMEM((here, 8), jnp.int32),
+            pltpu.SMEM((here, 8), jnp.int32),
+            pltpu.SMEM((here, 8), jnp.int32),
+            pltpu.VMEM(inputs.shape, BF),
+            pltpu.VMEM((9 * chans, chans), BF),
+            pltpu.VMEM((1, chans), F32),
+            pltpu.VMEM((3 * chans, 3 * chans), BF),
+            pltpu.VMEM((5 * block, 64, chans), BF),
+            pltpu.VMEM((here, 36, 32, chans), F32),
+            pltpu.VMEM((here, 36, 16, chans), BF),
+            pltpu.VMEM((here, 36, 16, chans), BF),
+            pltpu.VMEM((near, block, 64, chans), BF),
             pltpu.VMEM((5 * block, 64, chans), BF),
             pltpu.VMEM((here * 8, 64, chans), F32),
             pltpu.SMEM((here * 8,), jnp.int32),
@@ -564,21 +602,12 @@
             pltpu.VMEM((plane, rows, chans), BF),
             pltpu.VMEM((plane - 1, rows, chans), BF),
             pltpu.VMEM((nz, rows, chans), F32),
-            dma((len(NEAR),)),
-            dma((len(NEAR),)),
-            dma,
-            dma,
-            dma((plane - 1,)),
-            dma((plane - 1,)),
-            dma((nz - 1,)),
-            dma((nz - 1,)),
-            dma((plane - 1,)),
-            dma((plane - 1,)),
-            dma,
-            dma,
-        ],
+            dma((6 + here,)),
+            dma((3,)),
+        ]
+        + [dma if n is None else dma((n,)) for n in wires for _ in range(2)],
         compiler_params=pltpu.CompilerParams(
-            collective_id=0, has_side_effects=True, vmem_limit_bytes=26 * 2**20
+            collective_id=0, has_side_effects=True, vmem_limit_bytes=56 * 2**20
         ),
     )(
         neighbours,
@@ -586,18 +615,32 @@
         corners,
         inputs,
         cotangent,
-        flat,
+        weights.reshape(9 * chans, chans),
         bias_vector.reshape(1, chans),
-        pool,
-        center,
-        zl,
-        zr,
     )
-    main = fin[:, 0:mr].reshape(8 * chans, chans)
-    rest = fin[:, mr : mr + tr].reshape(chans, chans)
-    weight_grad = jnp.concatenate([main, rest], axis=0).astype(F32)
-    bias_grad = fin[0, mr + tr].astype(F32) + fin[0, mr + tr + 1].astype(F32)
-    return (outputs, input_grad, weight_grad.reshape(weights.shape), bias_grad)
+    outputs, input_grad, weight_grad, bias_grad = pl.pallas_call(
+        functools.partial(write_kernel, mr, tr),
+        out_shape=(
+            jax.ShapeDtypeStruct(inputs.shape, BF),
+            jax.ShapeDtypeStruct(inputs.shape, BF),
+            jax.ShapeDtypeStruct((9 * chans, chans), F32),
+            jax.ShapeDtypeStruct((1, chans), F32),
+        ),
+        in_specs=[hbm] * 3,
+        out_specs=(hbm, hbm, hbm, vmem),
+        scratch_shapes=[
+            pltpu.VMEM((2 * plane, rows, chans), BF),
+            pltpu.VMEM((9 * chans, chans), F32),
+            dma((2 + 2 * here,)),
+        ],
+        compiler_params=pltpu.CompilerParams(vmem_limit_bytes=56 * 2**20),
+    )(outputs, input_grad, fin)
+    return (
+        outputs,
+        input_grad,
+        weight_grad.reshape(weights.shape),
+        bias_grad.reshape(bias_vector.shape),
+    )
 
 
 def solution(mesh):

time: 69.4 us -> 108 us (1.56)
  Pallas kernels: 61.9 us -> 107 us
  local copies, waits for them, and re-layouts: 5.06 us -> 0 us
  other arithmetic: 1.4 us -> 0 us
    pallas_call x2, Pallas kernels: 61.9 us -> 107 us  [the longest x1 58 us: body(): pl.pallas_call(functools.partial(main_kernel, sizes, factor), out_shape=(...]
    unnamed x22 -> x0, local copies, waits for them, and re-layouts: 5.02 us -> none
where the time goes in v3:
time: 108 us
  Pallas kernels  107 us (99%)
    pallas_call x1, Pallas kernels, body(): pl.pallas_call(functools.partial(main_kernel, sizes, factor), out_shape=(...  58 us
    pallas_call x1, Pallas kernels, body(): pl.pallas_call(functools.partial(write_kernel, mr, tr), out_shape=(jax.Sh...  49.3 us

profile of v3, /device:TPU:1, one launch (start us, length us, event | category | flops | bytes accessed | tf_op | source)
XLA Modules:
  0.0 108.0 jit_solution(9325464271076571917)
XLA Ops:
  0.6 58.0 %shard_map.102 = (bf16[3,32,32,128]{3,2,1,0:T(8,128)(2,1)}, bf16[3,32,32,128]{3,2,1,0:T(8,128)(2,1)}, bf16[64,24,128]{2,1,0:T(8,128)(2,1)}) custom-call(s32[3,8]{1,0:T(4,128)} %nb_in.1, s32[3,8]{1,0:T(4,128)} %rot_in.1, s32[3,8]{1,0:T(4,128)} %cor_in.1, bf16[3,32,32,128]{3,2,1,0:T(8,128)(2,1)} %inp_in.1, bf16[3,32,32,128]{3,2,1,0:T(8,128)(2,1)} %cot_in.1, ...), custom_call_target="tpu_custom_call" | custom-call | tf_op jit(solution)/shard_map/pallas_call | solution.py:569
  58.7 49.3 %shard_map.103 = (bf16[3,32,32,128]{3,2,1,0:T(8,128)(2,1)}, bf16[3,32,32,128]{3,2,1,0:T(8,128)(2,1)}, f32[1152,128]{1,0:T(8,128)}, f32[1,128]{1,0:T(1,128)}) custom-call(bf16[3,32,32,128]{3,2,1,0:T(8,128)(2,1)} %get-tuple-element.11.out, bf16[3,32,32,128]{3,2,1,0:T(8,128)(2,1)} %get-tuple-element.12.ingrad, bf16[64,24,128]{2,1,0:T(8,128)(2,1)} %get-tuple-element.13.fin_o), custom_call_target="tpu_custom_call" | custom-call | tf_op jit(solution)/shard_map/pallas_call | solution.py:621

commit v4 on v3

--- a/solution.py
+++ b/solution.py
@@ -526,29 +526,36 @@
 
 
 def write_kernel(
-    mr, tr, out, ingrad, fin_o, out_o, ingrad_o, wgrad_o, bgrad, fin, wide, sems
+    mr, tr, out, ingrad, fin_o, out_o, ingrad_o, wgrad_o, bgrad, fin, held, wide, sems
 ):
     here = out.shape[0]
     load = pltpu.make_async_copy(fin_o, fin, sems.at[0])
     load.start()
-    moves = []
+    loads, stores = [], []
     for p in range(here):
         for n, (src, dst) in enumerate(((out, out_o), (ingrad, ingrad_o))):
-            moves.append(
-                pltpu.make_async_copy(src.at[p], dst.at[p], sems.at[2 + 2 * p + n])
+            at = 2 * p + n
+            loads.append(
+                pltpu.make_async_copy(src.at[p], held.at[at], sems.at[2 + 2 * at])
             )
-            moves[-1].start()
+            stores.append(
+                pltpu.make_async_copy(held.at[at], dst.at[p], sems.at[3 + 2 * at])
+            )
+            loads[-1].start()
     load.wait()
     slabs = fin.shape[0]
     wide[0:1024] = fin[:, 0:mr].astype(F32).reshape(1024, 128)
     for s in range(slabs):
         tail = fin[s, mr:].astype(F32)
         wide[1024 + tr * s : 1024 + tr * (s + 1)] = tail[0:tr]
-    moves.append(pltpu.make_async_copy(wide, wgrad_o, sems.at[1]))
-    moves[-1].start()
+    stores.append(pltpu.make_async_copy(wide, wgrad_o, sems.at[1]))
+    stores[-1].start()
     tail = fin[0, mr:].astype(F32)
     bgrad[...] = tail[tr : tr + 1] + tail[tr + 1 : tr + 2]
-    for c in moves:
+    for c, d in zip(loads, stores):
+        c.wait()
+        d.start()
+    for c in stores:
         c.wait()
 
 
@@ -630,8 +637,9 @@
         out_specs=(hbm, hbm, hbm, vmem),
         scratch_shapes=[
             pltpu.VMEM((2 * plane, rows, chans), BF),
+            pltpu.VMEM((2 * here, length, length, chans), BF),
             pltpu.VMEM((9 * chans, chans), F32),
-            dma((2 + 2 * here,)),
+            dma((2 + 4 * here,)),
         ],
         compiler_params=pltpu.CompilerParams(vmem_limit_bytes=56 * 2**20),
     )(outputs, input_grad, fin)

time: 108 us -> 61.8 us (0.57)
  Pallas kernels: 107 us -> 61 us
    pallas_call x1, Pallas kernels: 49.3 us -> 3.01 us  [body(): pl.pallas_call(functools.partial(write_kernel, mr, tr), out_shape=(jax.Sh...]
where the time goes in v4:
time: 61.8 us; the launch traced here: 61.7 us
  Pallas kernels  61 us (99%)
  between operations  0.64 us (1%)
    pallas_call x1, Pallas kernels, body(): pl.pallas_call(functools.partial(main_kernel, sizes, factor), out_shape=(...  58 us
    pallas_call x1, Pallas kernels, body(): pl.pallas_call(functools.partial(write_kernel, mr, tr), out_shape=(jax.Sh...  3.01 us

profile of v4, /device:TPU:1, one launch (start us, length us, event | category | flops | bytes accessed | tf_op | source)
XLA Modules:
  0.0 61.7 jit_solution(5558309494936411268)
XLA Ops:
  0.6 58.0 %shard_map.102 = (bf16[3,32,32,128]{3,2,1,0:T(8,128)(2,1)}, bf16[3,32,32,128]{3,2,1,0:T(8,128)(2,1)}, bf16[64,24,128]{2,1,0:T(8,128)(2,1)}) custom-call(s32[3,8]{1,0:T(4,128)} %nb_in.1, s32[3,8]{1,0:T(4,128)} %rot_in.1, s32[3,8]{1,0:T(4,128)} %cor_in.1, bf16[3,32,32,128]{3,2,1,0:T(8,128)(2,1)} %inp_in.1, bf16[3,32,32,128]{3,2,1,0:T(8,128)(2,1)} %cot_in.1, ...), custom_call_target="tpu_custom_call" | custom-call | tf_op jit(solution)/shard_map/pallas_call | solution.py:576
  58.7 3.0 %shard_map.103 = (bf16[3,32,32,128]{3,2,1,0:T(8,128)(2,1)}, bf16[3,32,32,128]{3,2,1,0:T(8,128)(2,1)}, f32[1152,128]{1,0:T(8,128)}, f32[1,128]{1,0:T(1,128)}) custom-call(bf16[3,32,32,128]{3,2,1,0:T(8,128)(2,1)} %get-tuple-element.11.out, bf16[3,32,32,128]{3,2,1,0:T(8,128)(2,1)} %get-tuple-element.12.ingrad, bf16[64,24,128]{2,1,0:T(8,128)(2,1)} %get-tuple-element.13.fin_o), custom_call_target="tpu_custom_call" | custom-call | tf_op jit(solution)/shard_map/pallas_call | solution.py:628

commit v5 on v4

--- a/solution.py
+++ b/solution.py
@@ -134,17 +134,19 @@
     y = lax.rem(me // 2, ny)
     x = lax.rem(me // (2 * ny), nx)
     z = me // (2 * ny * nx)
-    q = x * ny + y
+    u, u_step = y + core * (z - y), 2 + core * (2 * plane - 2)
+    v, v_step = z + core * (y - z), 2 * plane + core * (2 - 2 * plane)
+    q = x * ny + u
     mate = me + 1 - 2 * core
     block = here * 4
     mr, tr = 1024 // (2 * plane), 128 // (2 * plane)
 
     def peer_of(k):
-        qk = lax.rem(x + k // ny, nx) * ny + lax.rem(y + lax.rem(k, ny), ny)
-        return qk, me + 2 * (qk - q)
-
-    def z_peer(k):
-        return me + 2 * plane * (lax.rem(z + k, nz) - z)
+        xk, uk = lax.rem(x + k // ny, nx), lax.rem(u + lax.rem(k, ny), ny)
+        return xk * ny + uk, me + 2 * ny * (xk - x) + u_step * (uk - u)
+
+    def v_peer(k):
+        return me + v_step * (lax.rem(v + k, nz) - v)
 
     def near(o):
         return lax.rem(me + o + count, count)
@@ -169,7 +171,7 @@
         return carry
 
     for k in range(1, nz):
-        greet(z_peer(k))
+        greet(v_peer(k))
     lax.fori_loop(1, plane, greet_plane, 0)
     for o in NEAR:
         greet(near(o))
@@ -424,10 +426,10 @@
         p_reduce(k).wait_recv()
         return c + p_in[k - 1].astype(F32)
 
-    z_all[z] = every(p_add, wloc[core * plane + q] + core_in[q])
+    z_all[v] = every(p_add, wloc[core * plane + q] + core_in[q])
 
     def z_gather(k):
-        return copy(z_all.at[z], z_all.at[z], s_z.at[k - 1], r_z.at[k - 1], z_peer(k))
+        return copy(z_all.at[v], z_all.at[v], s_z.at[k - 1], r_z.at[k - 1], v_peer(k))
 
     for k in range(1, nz):
         z_gather(k).start()

time: 61.8 us -> 60.9 us (0.985)
  Pallas kernels: 61 us -> 60 us
    pallas_call x1, Pallas kernels: 58 us -> 57 us  [body(): pl.pallas_call(functools.partial(main_kernel, sizes, factor), out_shape=(...]
where the time goes in v5:
time: 60.9 us; the launch traced here: 60.7 us
  Pallas kernels  60 us (99%)
  between operations  0.64 us (1%)
    pallas_call x1, Pallas kernels, body(): pl.pallas_call(functools.partial(main_kernel, sizes, factor), out_shape=(...  57 us
    pallas_call x1, Pallas kernels, body(): pl.pallas_call(functools.partial(write_kernel, mr, tr), out_shape=(jax.Sh...  3.01 us

profile of v5, /device:TPU:1, one launch (start us, length us, event | category | flops | bytes accessed | tf_op | source)
XLA Modules:
  0.0 60.7 jit_solution(17488542612064678122)
XLA Ops:
  0.6 57.0 %shard_map.102 = (bf16[3,32,32,128]{3,2,1,0:T(8,128)(2,1)}, bf16[3,32,32,128]{3,2,1,0:T(8,128)(2,1)}, bf16[64,24,128]{2,1,0:T(8,128)(2,1)}) custom-call(s32[3,8]{1,0:T(4,128)} %nb_in.1, s32[3,8]{1,0:T(4,128)} %rot_in.1, s32[3,8]{1,0:T(4,128)} %cor_in.1, bf16[3,32,32,128]{3,2,1,0:T(8,128)(2,1)} %inp_in.1, bf16[3,32,32,128]{3,2,1,0:T(8,128)(2,1)} %cot_in.1, ...), custom_call_target="tpu_custom_call" | custom-call | tf_op jit(solution)/shard_map/pallas_call | solution.py:578
  57.7 3.0 %shard_map.103 = (bf16[3,32,32,128]{3,2,1,0:T(8,128)(2,1)}, bf16[3,32,32,128]{3,2,1,0:T(8,128)(2,1)}, f32[1152,128]{1,0:T(8,128)}, f32[1,128]{1,0:T(1,128)}) custom-call(bf16[3,32,32,128]{3,2,1,0:T(8,128)(2,1)} %get-tuple-element.11.out, bf16[3,32,32,128]{3,2,1,0:T(8,128)(2,1)} %get-tuple-element.12.ingrad, bf16[64,24,128]{2,1,0:T(8,128)(2,1)} %get-tuple-element.13.fin_o), custom_call_target="tpu_custom_call" | custom-call | tf_op jit(solution)/shard_map/pallas_call | solution.py:630

commit v6 on v5

--- a/solution.py
+++ b/solution.py
@@ -268,7 +268,7 @@
         center[p, pl.ds(y0, 6)] = total
         return carry
 
-    lax.fori_loop(0, here * 3, spread_back, 0)
+    lax.fori_loop(0, here * 4, spread_back, 0)
     for c in edges:
         c.wait_recv()
 
@@ -360,7 +360,7 @@
         out[p, pl.ds(i0, 8)] = (dot(lhs, w[...]) + bias[...]).astype(BF).reshape(8, 32, 128)
         return carry
 
-    lax.fori_loop(here * 3, here * 4, spread_back, 0)
+    lax.fori_loop(here * 4, here * 5, spread_back, 0)
     swap.wait_recv()
 
     half = (nx // 2) * ny + ny // 2
@@ -385,7 +385,7 @@
         return c
 
     every(p_start, 0)
-    lax.fori_loop(here * 4, here * 6, spread_back, 0)
+    lax.fori_loop(here * 5, here * 6, spread_back, 0)
 
     def last_two(step, c):
         return jnp.where(c >= 30, step + c - 30, -1)
@@ -420,7 +420,21 @@
         return carry
 
     lax.fori_loop(0, here, turn_back, 0)
-    lax.fori_loop(0, 5 * block, gather_terms, 0)
+    backs = []
+    for n, o in enumerate(NEAR):
+        first = (REACH + o) * block
+        lax.fori_loop(first, first + block, gather_terms, 0)
+        backs.append(
+            copy(
+                terms.at[pl.ds(first, block)],
+                arr.at[n],
+                s_term.at[n],
+                r_term.at[n],
+                near(o),
+            )
+        )
+        backs[n].start()
+    lax.fori_loop(own, own + block, gather_terms, 0)
 
     def p_add(k, c):
         p_reduce(k).wait_recv()
@@ -433,19 +447,6 @@
 
     for k in range(1, nz):
         z_gather(k).start()
-    backs = [
-        copy(
-            terms.at[pl.ds((REACH + o) * block, block)],
-            arr.at[n],
-            s_term.at[n],
-            r_term.at[n],
-            near(o),
-        )
-        for n, o in enumerate(NEAR)
-    ]
-    for c in backs:
-        c.start()
-
     lax.fori_loop(0, 4 * here, conv, 0)
     stores = [pltpu.make_async_copy(out, out_o, s_store.at[0])]
     stores[0].start()
@@ -544,6 +545,9 @@
                 pltpu.make_async_copy(held.at[at], dst.at[p], sems.at[3 + 2 * at])
             )
             loads[-1].start()
+    for c, d in zip(loads, stores):
+        c.wait()
+        d.start()
     load.wait()
     slabs = fin.shape[0]
     wide[0:1024] = fin[:, 0:mr].astype(F32).reshape(1024, 128)
@@ -554,9 +558,6 @@
     stores[-1].start()
     tail = fin[0, mr:].astype(F32)
     bgrad[...] = tail[tr : tr + 1] + tail[tr + 1 : tr + 2]
-    for c, d in zip(loads, stores):
-        c.wait()
-        d.start()
     for c in stores:
         c.wait()
 

time: 60.9 us -> 59 us (0.969)
  Pallas kernels: 60 us -> 58.2 us
    pallas_call x1, Pallas kernels: 57 us -> 55.1 us  [body(): pl.pallas_call(functools.partial(main_kernel, sizes, factor), out_shape=(...]
where the time goes in v6:
time: 59 us; the launch traced here: 58.8 us
  Pallas kernels  58.2 us (99%)
  between operations  0.64 us (1%)
    pallas_call x1, Pallas kernels, body(): pl.pallas_call(functools.partial(main_kernel, sizes, factor), out_shape=(...  55.1 us
    pallas_call x1, Pallas kernels, body(): pl.pallas_call(functools.partial(write_kernel, mr, tr), out_shape=(jax.Sh...  3.03 us

profile of v6, /device:TPU:1, one launch (start us, length us, event | category | flops | bytes accessed | tf_op | source)
XLA Modules:
  0.0 58.8 jit_solution(7475386998358659460)
XLA Ops:
  0.6 55.1 %shard_map.102 = (bf16[3,32,32,128]{3,2,1,0:T(8,128)(2,1)}, bf16[3,32,32,128]{3,2,1,0:T(8,128)(2,1)}, bf16[64,24,128]{2,1,0:T(8,128)(2,1)}) custom-call(s32[3,8]{1,0:T(4,128)} %nb_in.1, s32[3,8]{1,0:T(4,128)} %rot_in.1, s32[3,8]{1,0:T(4,128)} %cor_in.1, bf16[3,32,32,128]{3,2,1,0:T(8,128)(2,1)} %inp_in.1, bf16[3,32,32,128]{3,2,1,0:T(8,128)(2,1)} %cot_in.1, ...), custom_call_target="tpu_custom_call" | custom-call | tf_op jit(solution)/shard_map/pallas_call | solution.py:579
  55.8 3.0 %shard_map.103 = (bf16[3,32,32,128]{3,2,1,0:T(8,128)(2,1)}, bf16[3,32,32,128]{3,2,1,0:T(8,128)(2,1)}, f32[1152,128]{1,0:T(8,128)}, f32[1,128]{1,0:T(1,128)}) custom-call(bf16[3,32,32,128]{3,2,1,0:T(8,128)(2,1)} %get-tuple-element.11.out, bf16[3,32,32,128]{3,2,1,0:T(8,128)(2,1)} %get-tuple-element.12.ingrad, bf16[64,24,128]{2,1,0:T(8,128)(2,1)} %get-tuple-element.13.fin_o), custom_call_target="tpu_custom_call" | custom-call | tf_op jit(solution)/shard_map/pallas_call | solution.py:631

commit v7 on v6

--- a/solution.py
+++ b/solution.py
@@ -9,7 +9,7 @@
 from jax.sharding import PartitionSpec as P
 
 REACH = 2
-NEAR = (-2, -1, 1, 2)
+NEAR = (-2, 2, -1, 1)
 MESH = pl.DeviceIdType.MESH
 BF = jnp.bfloat16
 F32 = jnp.float32
@@ -360,7 +360,7 @@
         out[p, pl.ds(i0, 8)] = (dot(lhs, w[...]) + bias[...]).astype(BF).reshape(8, 32, 128)
         return carry
 
-    lax.fori_loop(here * 4, here * 5, spread_back, 0)
+    lax.fori_loop(here * 4, here * 6, spread_back, 0)
     swap.wait_recv()
 
     half = (nx // 2) * ny + ny // 2
@@ -385,7 +385,6 @@
         return c
 
     every(p_start, 0)
-    lax.fori_loop(here * 5, here * 6, spread_back, 0)
 
     def last_two(step, c):
         return jnp.where(c >= 30, step + c - 30, -1)

time: 59 us -> 57.4 us (0.973)
  Pallas kernels: 58.2 us -> 56.6 us
    pallas_call x1, Pallas kernels: 55.1 us -> 53.5 us  [body(): pl.pallas_call(functools.partial(main_kernel, sizes, factor), out_shape=(...]
where the time goes in v7:
time: 57.4 us; the launch traced here: 57.2 us
  Pallas kernels  56.6 us (99%)
  between operations  0.64 us (1%)
    pallas_call x1, Pallas kernels, body(): pl.pallas_call(functools.partial(main_kernel, sizes, factor), out_shape=(...  53.5 us
    pallas_call x1, Pallas kernels, body(): pl.pallas_call(functools.partial(write_kernel, mr, tr), out_shape=(jax.Sh...  3.03 us

profile of v7, /device:TPU:1, one launch (start us, length us, event | category | flops | bytes accessed | tf_op | source)
XLA Modules:
  0.0 57.2 jit_solution(5817619004929462713)
XLA Ops:
  0.6 53.5 %shard_map.102 = (bf16[3,32,32,128]{3,2,1,0:T(8,128)(2,1)}, bf16[3,32,32,128]{3,2,1,0:T(8,128)(2,1)}, bf16[64,24,128]{2,1,0:T(8,128)(2,1)}) custom-call(s32[3,8]{1,0:T(4,128)} %nb_in.1, s32[3,8]{1,0:T(4,128)} %rot_in.1, s32[3,8]{1,0:T(4,128)} %cor_in.1, bf16[3,32,32,128]{3,2,1,0:T(8,128)(2,1)} %inp_in.1, bf16[3,32,32,128]{3,2,1,0:T(8,128)(2,1)} %cot_in.1, ...), custom_call_target="tpu_custom_call" | custom-call | tf_op jit(solution)/shard_map/pallas_call | solution.py:578
  54.2 3.0 %shard_map.103 = (bf16[3,32,32,128]{3,2,1,0:T(8,128)(2,1)}, bf16[3,32,32,128]{3,2,1,0:T(8,128)(2,1)}, f32[1152,128]{1,0:T(8,128)}, f32[1,128]{1,0:T(1,128)}) custom-call(bf16[3,32,32,128]{3,2,1,0:T(8,128)(2,1)} %get-tuple-element.11.out, bf16[3,32,32,128]{3,2,1,0:T(8,128)(2,1)} %get-tuple-element.12.ingrad, bf16[64,24,128]{2,1,0:T(8,128)(2,1)} %get-tuple-element.13.fin_o), custom_call_target="tpu_custom_call" | custom-call | tf_op jit(solution)/shard_map/pallas_call | solution.py:630
